TPU v7x, 256 devices: a whole 4x4x8 slice. The times are simulated.
256 devices in a mesh: frame: 32 (over x, y, core), head: 8 (over z).
Axes of the slice: x: 4, y: 4, z: 8, core: 2. Of those that a mesh axis runs over, the one named last changes fastest.
Arguments:
- queries: bfloat16 [7168, 3072], P('frame', 'head'), may hold values from -24 to 24
- key_rows: bfloat16 [7168, 3072], P('frame', 'head'), may hold values from -24 to 24
- value_rows: bfloat16 [7168, 3072], P('frame', 'head'), may hold values from -5 to 5
- ref_keys: bfloat16 [32, 1024, 3072], P('frame', None, 'head'), may hold values from -5 to 5
- ref_values: bfloat16 [32, 1024, 3072], P('frame', None, 'head'), may hold values from -5 to 5
- key_lists: int32 [32, 8], P('frame'), may hold values from 0 to 31, as said below
- list_counts: int32 [32], P('frame'), may hold values from 1 to 8, as said below
- owner_index: int32 [1], replicated, may hold values from 0 to 31
- out_weight: bfloat16 [3072, 3072], P('head'), may hold values from -1.5 to 1.5
- residual: bfloat16 [7168, 3072], P('frame', 'head'), may hold values from -3 to 3
- gate_scale: float32 [3072], P('head'), may hold values from 0.5 to 2
Outputs:
- block_out: bfloat16 [7168, 3072], P('frame', 'head')
Inputs may be any that keep to these rules, and one draw needn't show every extreme that they name: `key_lists`: the first list_counts[f] entries of row f are distinct frames other than f, each within 4 frames of f; the remaining entries equal f. `list_counts`: some frame lists every frame within 4 of it.
All inputs are finite; a program needn't handle non-finite values.
Results may differ from a plain program's by a relative error of at most 0.02.
Values may be sent and summed in bfloat16 or wider, within the bound.
A program may use at most 64 MiB of HBM per device.

v0:
```python
import math

import jax
import jax.numpy as jnp
from jax import lax
from jax.sharding import PartitionSpec as P

HD = 128
REACH = 4


def broadcast(block, axis, source):
    block = jnp.where(lax.axis_index(axis) == source, block, jnp.zeros_like(block))
    return lax.psum(block, axis)


def from_behind(block, axis, distance):
    devices = range(lax.axis_size(axis))
    route = [(i - distance, i) for i in devices if i - distance in devices]
    return lax.ppermute(block, axis, route)


def absorb(carried, query_heads, key_block, value_block, allowed):
    running_max, running_sum, weighted = carried
    head_count = query_heads.shape[1]
    key_heads = key_block.reshape(key_block.shape[0], head_count, HD)
    value_heads = value_block.reshape(value_block.shape[0], head_count, HD)
    scores = jnp.einsum(
        "qhd,khd->hqk", query_heads, key_heads, preferred_element_type=jnp.float32
    ) * (1.0 / math.sqrt(HD))
    if allowed is not None:
        scores = jnp.where(allowed[None, None, :], scores, -jnp.inf)
    new_max = jnp.maximum(running_max, jnp.max(scores, axis=-1))
    factor = jnp.exp(running_max - new_max)
    weights = jnp.exp(scores - new_max[:, :, None])
    running_sum = running_sum * factor + jnp.sum(weights, axis=-1)
    weighted = weighted * factor.T[:, :, None] + jnp.einsum(
        "hqk,khd->qhd",
        weights.astype(jnp.bfloat16),
        value_heads,
        preferred_element_type=jnp.float32,
    )
    return (new_max, running_sum, weighted)


def frame_block(carried, query_heads, key_block, value_block, begin_row, listed, live_slots):
    frame_of = (begin_row + jnp.arange(key_block.shape[0], dtype=jnp.int32)) // query_heads.shape[0]
    allowed = jnp.any((frame_of[:, None] == listed[None, :]) & live_slots[None, :], axis=1)
    return lax.cond(
        jnp.any(allowed),
        lambda current: absorb(current, query_heads, key_block, value_block, allowed),
        lambda current: current,
        carried,
    )


def per_device(
    queries,
    key_rows,
    value_rows,
    ref_keys,
    ref_values,
    key_lists,
    list_counts,
    owner_index,
    out_weight,
    residual,
    gate_scale,
):
    frame_len = queries.shape[0]
    columns_here = queries.shape[1]
    head_count = columns_here // HD
    query_heads = queries.reshape(frame_len, head_count, HD)
    listed = key_lists[0]
    live_slots = jnp.arange(listed.shape[0], dtype=jnp.int32) < list_counts[0]
    position = lax.axis_index("frame")
    carried = (
        jnp.full((head_count, frame_len), -jnp.inf, jnp.float32),
        jnp.zeros((head_count, frame_len), jnp.float32),
        jnp.zeros((frame_len, head_count, HD), jnp.float32),
    )
    style_keys, style_values = (
        broadcast(ref_keys, "frame", owner_index[0]),
        broadcast(ref_values, "frame", owner_index[0]),
    )
    carried = absorb(carried, query_heads, style_keys[0], style_values[0], None)
    carried = absorb(carried, query_heads, key_rows, value_rows, None)
    for offset in list(range(1, REACH + 1)) + list(range(-REACH, 0)):
        moved_keys, moved_values = from_behind((key_rows, value_rows), "frame", offset)
        carried = frame_block(
            carried,
            query_heads,
            moved_keys,
            moved_values,
            (position - offset) * frame_len,
            listed,
            live_slots,
        )
    running_max, running_sum, weighted = carried
    attended = (
        (weighted / running_sum.T[:, :, None]).astype(jnp.bfloat16).reshape(frame_len, columns_here)
    )
    shares = lax.psum_scatter(
        lax.dot_general(
            out_weight, attended, (((0,), (1,)), ((), ())), preferred_element_type=jnp.float32
        ).astype(jnp.bfloat16),
        "head",
        scatter_dimension=0,
        tiled=True,
    ).astype(jnp.float32)
    return (residual.astype(jnp.float32) + gate_scale[None, :] * shares.T).astype(jnp.bfloat16)


def solution(mesh):
    placed = (
        P("frame", "head"),
        P("frame", "head"),
        P("frame", "head"),
        P("frame", None, "head"),
        P("frame", None, "head"),
        P("frame", None),
        P("frame"),
        P(),
        P("head", None),
        P("frame", "head"),
        P("head"),
    )
    return jax.shard_map(
        per_device, mesh=mesh, in_specs=placed, out_specs=P("frame", "head"), check_vma=False
    )
```

profile of v0, /device:TPU:8, one launch (start us, length us, event | category | flops | bytes accessed | tf_op | source)
XLA Modules:
  0.0 268.2 jit_solution(7305506349866342035)
XLA Ops:
  6.5 1.9 copy.128
  8.4 1.9 collective-permute-start
  10.3 3.5 %collective-permute-start.2 = (bf16[224,384]{0,1:T(8,128)(2,1)}, bf16[224,384]{0,1:T(8,128)(2,1)}, u32[]{:S(2)}, u32[]{:S(2)}) collective-permute-start(bf16[224,384]{0,1:T(8,128)(2,1)} %copy.128), channel_id=1, source_target_pairs={{0,16},{8,24},{16,32},{24,40},{32,48},{40,56},{48,64},{56,72},{64,... | collective-permute-start | bytes 516104 | tf_op jit(solution)/shard_map/ppermute | solution.py:20
  13.8 1.1 copy.133
  14.9 3.0 %collective-permute-start.1 = (bf16[224,384]{0,1:T(8,128)(2,1)S(1)}, bf16[224,384]{0,1:T(8,128)(2,1)}, u32[]{:S(2)}, u32[]{:S(2)}) collective-permute-start(bf16[224,384]{0,1:T(8,128)(2,1)S(1)} %copy.133), channel_id=1, source_target_pairs={{0,8},{8,16},{16,24},{24,32},{32,40},{40,48},{48,56},{56,64},{64,7... | collective-permute-start | bytes 516104 | tf_op jit(solution)/shard_map/ppermute | solution.py:20
  17.9 3.1 %collective-permute-start.3 = (bf16[224,384]{0,1:T(8,128)(2,1)S(1)}, bf16[224,384]{0,1:T(8,128)(2,1)}, u32[]{:S(2)}, u32[]{:S(2)}) collective-permute-start(bf16[224,384]{0,1:T(8,128)(2,1)S(1)} %copy.133), channel_id=1, source_target_pairs={{0,16},{8,24},{16,32},{24,40},{32,48},{40,56},{48,64},{56,72},{64,... | collective-permute-start | bytes 516104 | tf_op jit(solution)/shard_map/ppermute | solution.py:20
  21.0 3.8 %collective-permute-start.4 = (bf16[224,384]{0,1:T(8,128)(2,1)}, bf16[224,384]{0,1:T(8,128)(2,1)}, u32[]{:S(2)}, u32[]{:S(2)}) collective-permute-start(bf16[224,384]{0,1:T(8,128)(2,1)} %copy.128), channel_id=1, source_target_pairs={{0,24},{8,32},{16,40},{24,48},{32,56},{40,64},{48,72},{56,80},{64,... | collective-permute-start | bytes 516104 | tf_op jit(solution)/shard_map/ppermute | solution.py:20
  25.4 2.3 copy.124
  27.7 1.2 copy.131
  28.9 1.0 broadcast_select_fusion
  29.9 2.3 copy.125
  32.2 1.2 copy.132
  33.4 1.1 copy.126
  35.2 1.5 fusion.89
  41.6 2.1 fusion.105
  43.7 107.6 %all-reduce.3.cloned.1.call-done = (bf16[1024,3,128]{2,0,1:T(8,128)(2,1)}, bf16[1024,3,128]{2,0,1:T(8,128)(2,1)}) async-done(((bf16[1024,3,128]{2,0,1:T(8,128)(2,1)}, bf16[1024,3,128]{2,0,1:T(8,128)(2,1)}), (bf16[1024,3,128]{2,0,1:T(8,128)(2,1)}, bf16[1024,3,128]{2,0,1:T(8,128)(2,1)})) %all-reduce.3.cloned.1.call-update) | async-done | bytes 1572880 | tf_op jit(solution)/shard_map/psum | solution.py:14
  151.4 1.9 bitcast_reduce_fusion
  153.3 1.0 fusion.71
  154.3 3.0 %collective-permute-start.5 = (bf16[224,384]{0,1:T(8,128)(2,1)S(1)}, bf16[224,384]{0,1:T(8,128)(2,1)S(1)}, u32[]{:S(2)}, u32[]{:S(2)}) collective-permute-start(bf16[224,384]{0,1:T(8,128)(2,1)S(1)} %copy.133), channel_id=1, source_target_pairs={{0,24},{8,32},{16,40},{24,48},{32,56},{40,64},{48,72},{56,80},{64,... | collective-permute-start | bytes 516104 | tf_op jit(solution)/shard_map/ppermute | solution.py:20
  157.3 0.3 fusion.64
  157.6 4.3 %collective-permute-start.6 = (bf16[224,384]{0,1:T(8,128)(2,1)}, bf16[224,384]{0,1:T(8,128)(2,1)S(1)}, u32[]{:S(2)}, u32[]{:S(2)}) collective-permute-start(bf16[224,384]{0,1:T(8,128)(2,1)} %copy.128), channel_id=1, source_target_pairs={{0,32},{8,40},{16,48},{24,56},{32,64},{40,72},{48,80},{56,88},{64,... | collective-permute-start | bytes 516104 | tf_op jit(solution)/shard_map/ppermute | solution.py:20
  161.9 2.8 %collective-permute-start.7 = (bf16[224,384]{0,1:T(8,128)(2,1)S(1)}, bf16[224,384]{0,1:T(8,128)(2,1)S(1)}, u32[]{:S(2)}, u32[]{:S(2)}) collective-permute-start(bf16[224,384]{0,1:T(8,128)(2,1)S(1)} %copy.133), channel_id=1, source_target_pairs={{0,32},{8,40},{16,48},{24,56},{32,64},{40,72},{48,80},{56,88},{64,... | collective-permute-start | bytes 516104 | tf_op jit(solution)/shard_map/ppermute | solution.py:20
  164.7 1.3 collective-permute-start.8
  166.1 1.3 collective-permute-start.9
  167.4 0.7 copy-done.5
  168.0 1.3 collective-permute-start.10
  169.3 0.7 fusion.59
  170.1 1.3 collective-permute-start.11
  171.5 2.9 %collective-permute-start.12 = (bf16[224,384]{0,1:T(8,128)(2,1)}, bf16[224,384]{0,1:T(8,128)(2,1)}, u32[]{:S(2)}, u32[]{:S(2)}) collective-permute-start(bf16[224,384]{0,1:T(8,128)(2,1)} %copy.128), channel_id=1, source_target_pairs={{16,0},{24,8},{32,16},{40,24},{48,32},{56,40},{64,48},{72,56},{80,... | collective-permute-start | bytes 516104 | tf_op jit(solution)/shard_map/ppermute | solution.py:20
  174.3 1.7 collective-permute-done.8
  176.1 1.9 collective-permute-start.13
  178.0 2.3 collective-permute-done.9
  180.3 3.1 %collective-permute-start.14 = (bf16[224,384]{0,1:T(8,128)(2,1)}, bf16[224,384]{0,1:T(8,128)(2,1)}, u32[]{:S(2)}, u32[]{:S(2)}) collective-permute-start(bf16[224,384]{0,1:T(8,128)(2,1)} %copy.128), channel_id=1, source_target_pairs={{8,0},{16,8},{24,16},{32,24},{40,32},{48,40},{56,48},{64,56},{72,6... | collective-permute-start | bytes 516104 | tf_op jit(solution)/shard_map/ppermute | solution.py:20
  183.5 3.0 %collective-permute-done.10 = bf16[224,384]{0,1:T(8,128)(2,1)S(1)} collective-permute-done((bf16[224,384]{0,1:T(8,128)(2,1)}, bf16[224,384]{0,1:T(8,128)(2,1)S(1)}, u32[]{:S(2)}, u32[]{:S(2)}) %collective-permute-start.10) | collective-permute-done | bytes 172064 | tf_op jit(solution)/shard_map/ppermute | solution.py:20
  186.5 1.9 collective-permute-start.15
  188.4 2.8 %conditional.8 = ((f32[3,224]{1,0:T(4,128)S(1)}, f32[3,224]{1,0:T(4,128)S(1)}, f32[224,3,128]{2,0,1:T(8,128)S(1)})) conditional(s32[]{:T(128)} %convert_element_type.80, (f32[3,224]{1,0:T(4,128)S(1)}, f32[3,224]{1,0:T(4,128)S(1)}, f32[224,3,128]{2,0,1:T(8,128)S(1)}) %tuple.55, (pred[224]{0:T(512)(128)(4,1)S(1)}, bf16[224,384]{0,1:T(8,128)(2,1)}, ...), branch_computations={%region_15.16_spmd, %region_16.19_spmd} | conditional | flops 78298080 | bytes 3053824 | solution.py:49
  188.5 1.2 fusion.97
  189.7 0.1 fusion.3
  189.9 1.4 fusion.1
  191.3 2.8 %conditional.9 = ((f32[3,224]{1,0:T(4,128)S(1)}, f32[3,224]{1,0:T(4,128)S(1)}, f32[224,3,128]{2,0,1:T(8,128)S(1)})) conditional(s32[]{:T(128)} %convert_element_type.79, (f32[3,224]{1,0:T(4,128)S(1)}, f32[3,224]{1,0:T(4,128)S(1)}, f32[224,3,128]{2,0,1:T(8,128)S(1)}) %get-tuple-element.509, (pred[224]{0:T(512)(128)(4,1)S(1)}, ...), branch_computations={%region_20.21_spmd, %region_21.24_spmd} | conditional | flops 78298080 | bytes 3053824 | solution.py:49
  191.3 1.2 fusion.98
  192.5 0.1 fusion.10
  192.7 1.4 fusion.8
  194.1 2.8 %conditional.12 = ((f32[3,224]{1,0:T(4,128)S(1)}, f32[3,224]{1,0:T(4,128)S(1)}, f32[224,3,128]{2,0,1:T(8,128)S(1)})) conditional(s32[]{:T(128)} %convert_element_type.76, (f32[3,224]{1,0:T(4,128)S(1)}, f32[3,224]{1,0:T(4,128)S(1)}, f32[224,3,128]{2,0,1:T(8,128)S(1)}) %get-tuple-element.512, (pred[224]{0:T(512)(128)(4,1)S(1)}, ...), branch_computations={%region_35.36_spmd, %region_36.39_spmd} | conditional | flops 78298080 | bytes 3053824 | solution.py:49
  194.1 1.2 fusion.101
  195.4 0.1 fusion.31
  195.5 1.4 fusion.29
  196.9 2.8 %conditional.13 = ((f32[3,224]{1,0:T(4,128)S(1)}, f32[3,224]{1,0:T(4,128)S(1)}, f32[224,3,128]{2,0,1:T(8,128)S(1)})) conditional(s32[]{:T(128)} %convert_element_type.75, (f32[3,224]{1,0:T(4,128)S(1)}, f32[3,224]{1,0:T(4,128)S(1)}, f32[224,3,128]{2,0,1:T(8,128)S(1)}) %get-tuple-element.513, (pred[224]{0:T(512)(128)(4,1)S(1)}, ...), branch_computations={%region_40.41_spmd, %region_41.44_spmd} | conditional | flops 78298080 | bytes 3053824 | solution.py:49
  196.9 1.2 fusion.102
  198.2 0.1 fusion.38
  198.3 1.4 fusion.36
  199.7 2.8 %conditional.14 = ((f32[3,224]{1,0:T(4,128)S(1)}, f32[3,224]{1,0:T(4,128)S(1)}, f32[224,3,128]{2,0,1:T(8,128)S(1)})) conditional(s32[]{:T(128)} %convert_element_type.74, (f32[3,224]{1,0:T(4,128)S(1)}, f32[3,224]{1,0:T(4,128)S(1)}, f32[224,3,128]{2,0,1:T(8,128)S(1)}) %get-tuple-element.514, (pred[224,8]{0,1:T(8,128)(4,1)S(1)}, ...), branch_computations={%region_44.45_spmd, %region_45.49_spmd} | conditional | flops 78299648 | bytes 3055841 | solution.py:49
  199.8 1.2 fusion.103
  201.2 1.4 fusion.43
  202.6 1.9 conditional.15
  202.6 1.2 fusion.104
  204.0 0.4 fusion.50
  204.5 0.2 divide_convert_fusion
  204.6 0.1 copy.160
  204.8 2.0 fusion.56
  206.8 2.6 copy.198
  209.4 50.1 %reduce-scatter.4.cloned.1.call-done = bf16[384,224]{1,0:T(8,128)(2,1)} async-done(((bf16[3072,224]{1,0:T(8,128)(2,1)}), bf16[384,224]{1,0:T(8,128)(2,1)}) %reduce-scatter.4.cloned.1.call-update) | async-done | bytes 172048
  259.6 1.1 copy.199
  260.7 0.7 fusion.77
  (76 shorter events, 0.9 us)
Async XLA Ops:
  6.5 198.3 %copy-start = (bf16[384,3072]{1,0:T(8,128)(2,1)S(1)}, bf16[384,3072]{1,0:T(8,128)(2,1)}, u32[]{:S(2)}) copy-start(bf16[384,3072]{1,0:T(8,128)(2,1)} %param.35) | copy-start | bytes 7077892
  6.5 21.1 %copy-start.2 = (bf16[1,1024,384]{2,1,0:T(8,128)(2,1)S(1)}, bf16[1,1024,384]{2,1,0:T(8,128)(2,1)}, u32[]{:S(2)}) copy-start(bf16[1,1024,384]{2,1,0:T(8,128)(2,1)} %param.31) | copy-start | bytes 2359300
  6.5 144.8 %all-reduce.3.cloned.1.call-start = ((), (), s32[]{:S(2)}) async-start(), calls=%async_computation.2 | async-start | bytes 3145728 | tf_op jit(solution)/shard_map/psum | solution.py:14
  8.4 145.8 %collective-permute-start = (bf16[224,384]{0,1:T(8,128)(2,1)}, bf16[224,384]{0,1:T(8,128)(2,1)}, u32[]{:S(2)}, u32[]{:S(2)}) collective-permute-start(bf16[224,384]{0,1:T(8,128)(2,1)} %copy.128), channel_id=1, source_target_pairs={{0,8},{8,16},{16,24},{24,32},{32,40},{40,48},{48,56},{56,64},{64,7... | collective-permute-start | bytes 516104 | tf_op jit(solution)/shard_map/ppermute | solution.py:20
  10.3 151.5 %collective-permute-start.2 = (bf16[224,384]{0,1:T(8,128)(2,1)}, bf16[224,384]{0,1:T(8,128)(2,1)}, u32[]{:S(2)}, u32[]{:S(2)}) collective-permute-start(bf16[224,384]{0,1:T(8,128)(2,1)} %copy.128), channel_id=1, source_target_pairs={{0,16},{8,24},{16,32},{24,40},{32,48},{40,56},{48,64},{56,72},{64,... | collective-permute-start | bytes 516104 | tf_op jit(solution)/shard_map/ppermute | solution.py:20
  14.9 142.7 %collective-permute-start.1 = (bf16[224,384]{0,1:T(8,128)(2,1)S(1)}, bf16[224,384]{0,1:T(8,128)(2,1)}, u32[]{:S(2)}, u32[]{:S(2)}) collective-permute-start(bf16[224,384]{0,1:T(8,128)(2,1)S(1)} %copy.133), channel_id=1, source_target_pairs={{0,8},{8,16},{16,24},{24,32},{32,40},{40,48},{48,56},{56,64},{64,7... | collective-permute-start | bytes 516104 | tf_op jit(solution)/shard_map/ppermute | solution.py:20
  17.9 146.8 %collective-permute-start.3 = (bf16[224,384]{0,1:T(8,128)(2,1)S(1)}, bf16[224,384]{0,1:T(8,128)(2,1)}, u32[]{:S(2)}, u32[]{:S(2)}) collective-permute-start(bf16[224,384]{0,1:T(8,128)(2,1)S(1)} %copy.133), channel_id=1, source_target_pairs={{0,16},{8,24},{16,32},{24,40},{32,48},{40,56},{48,64},{56,72},{64,... | collective-permute-start | bytes 516104 | tf_op jit(solution)/shard_map/ppermute | solution.py:20
  21.0 145.1 %collective-permute-start.4 = (bf16[224,384]{0,1:T(8,128)(2,1)}, bf16[224,384]{0,1:T(8,128)(2,1)}, u32[]{:S(2)}, u32[]{:S(2)}) collective-permute-start(bf16[224,384]{0,1:T(8,128)(2,1)} %copy.128), channel_id=1, source_target_pairs={{0,24},{8,32},{16,40},{24,48},{32,56},{40,64},{48,72},{56,80},{64,... | collective-permute-start | bytes 516104 | tf_op jit(solution)/shard_map/ppermute | solution.py:20
  33.4 226.2 %reduce-scatter.4.cloned.1.call-start = ((), (), s32[]{:S(2)}) async-start(), calls=%async_computation.1 | async-start | bytes 1769472
  151.4 1.9 copy-start.13
  153.2 4.0 %copy-start.1 = (f32[3,224,224]{1,2,0:T(8,128)S(1)}, f32[3,224,224]{1,2,0:T(8,128)}, u32[]{:S(2)}) copy-start(f32[3,224,224]{1,2,0:T(8,128)} %get-tuple-element.450) | copy-start | bytes 1806340
  154.2 34.2 %copy-start.12 = (pred[224]{0:T(512)(128)(4,1)S(1)}, pred[224]{0:T(512)(128)(4,1)}, u32[]{:S(2)}) copy-start(pred[224]{0:T(512)(128)(4,1)} %get-tuple-element.394) | copy-start | bytes 676
  154.3 13.1 %collective-permute-start.5 = (bf16[224,384]{0,1:T(8,128)(2,1)S(1)}, bf16[224,384]{0,1:T(8,128)(2,1)S(1)}, u32[]{:S(2)}, u32[]{:S(2)}) collective-permute-start(bf16[224,384]{0,1:T(8,128)(2,1)S(1)} %copy.133), channel_id=1, source_target_pairs={{0,24},{8,32},{16,40},{24,48},{32,56},{40,64},{48,72},{56,80},{64,... | collective-permute-start | bytes 516104 | tf_op jit(solution)/shard_map/ppermute | solution.py:20
  157.6 12.5 %collective-permute-start.6 = (bf16[224,384]{0,1:T(8,128)(2,1)}, bf16[224,384]{0,1:T(8,128)(2,1)S(1)}, u32[]{:S(2)}, u32[]{:S(2)}) collective-permute-start(bf16[224,384]{0,1:T(8,128)(2,1)} %copy.128), channel_id=1, source_target_pairs={{0,32},{8,40},{16,48},{24,56},{32,64},{40,72},{48,80},{56,88},{64,... | collective-permute-start | bytes 516104 | tf_op jit(solution)/shard_map/ppermute | solution.py:20
  161.9 9.5 %collective-permute-start.7 = (bf16[224,384]{0,1:T(8,128)(2,1)S(1)}, bf16[224,384]{0,1:T(8,128)(2,1)S(1)}, u32[]{:S(2)}, u32[]{:S(2)}) collective-permute-start(bf16[224,384]{0,1:T(8,128)(2,1)S(1)} %copy.133), channel_id=1, source_target_pairs={{0,32},{8,40},{16,48},{24,56},{32,64},{40,72},{48,80},{56,88},{64,... | collective-permute-start | bytes 516104 | tf_op jit(solution)/shard_map/ppermute | solution.py:20
  164.7 11.3 %collective-permute-start.8 = (bf16[224,384]{0,1:T(8,128)(2,1)}, bf16[224,384]{0,1:T(8,128)(2,1)S(1)}, u32[]{:S(2)}, u32[]{:S(2)}) collective-permute-start(bf16[224,384]{0,1:T(8,128)(2,1)} %copy.128), channel_id=1, source_target_pairs={{32,0},{40,8},{48,16},{56,24},{64,32},{72,40},{80,48},{88,56},{96,... | collective-permute-start | bytes 516104 | tf_op jit(solution)/shard_map/ppermute | solution.py:20
  166.1 14.3 %collective-permute-start.9 = (bf16[224,384]{0,1:T(8,128)(2,1)S(1)}, bf16[224,384]{0,1:T(8,128)(2,1)S(1)}, u32[]{:S(2)}, u32[]{:S(2)}) collective-permute-start(bf16[224,384]{0,1:T(8,128)(2,1)S(1)} %copy.133), channel_id=1, source_target_pairs={{32,0},{40,8},{48,16},{56,24},{64,32},{72,40},{80,48},{88,56},{96,... | collective-permute-start | bytes 516104 | tf_op jit(solution)/shard_map/ppermute | solution.py:20
  167.4 0.7 copy-start.5
  168.0 18.4 %collective-permute-start.10 = (bf16[224,384]{0,1:T(8,128)(2,1)}, bf16[224,384]{0,1:T(8,128)(2,1)S(1)}, u32[]{:S(2)}, u32[]{:S(2)}) collective-permute-start(bf16[224,384]{0,1:T(8,128)(2,1)} %copy.128), channel_id=1, source_target_pairs={{24,0},{32,8},{40,16},{48,24},{56,32},{64,40},{72,48},{80,56},{88,... | collective-permute-start | bytes 516104 | tf_op jit(solution)/shard_map/ppermute | solution.py:20
  170.0 21.3 %copy-start.11 = (pred[224]{0:T(512)(128)(4,1)S(1)}, pred[224]{0:T(512)(128)(4,1)}, u32[]{:S(2)}) copy-start(pred[224]{0:T(512)(128)(4,1)} %get-tuple-element.396) | copy-start | bytes 676
  170.1 18.3 %copy-start.8 = (bf16[224,384]{0,1:T(8,128)(2,1)}, bf16[224,384]{0,1:T(8,128)(2,1)S(1)}, u32[]{:S(2)}) copy-start(bf16[224,384]{0,1:T(8,128)(2,1)S(1)} %collective-permute-done.6) | copy-start | bytes 516100
  170.1 26.8 %collective-permute-start.11 = (bf16[224,384]{0,1:T(8,128)(2,1)S(1)}, bf16[224,384]{0,1:T(8,128)(2,1)}, u32[]{:S(2)}, u32[]{:S(2)}) collective-permute-start(bf16[224,384]{0,1:T(8,128)(2,1)S(1)} %copy.133), channel_id=1, source_target_pairs={{24,0},{32,8},{40,16},{48,24},{56,32},{64,40},{72,48},{80,56},{88,... | collective-permute-start | bytes 516104 | tf_op jit(solution)/shard_map/ppermute | solution.py:20
  171.4 12.0 %copy-start.4 = (bf16[224,384]{0,1:T(8,128)(2,1)}, bf16[224,384]{0,1:T(8,128)(2,1)S(1)}, u32[]{:S(2)}) copy-start(bf16[224,384]{0,1:T(8,128)(2,1)S(1)} %collective-permute-done.7) | copy-start | bytes 516100
  171.5 28.3 %collective-permute-start.12 = (bf16[224,384]{0,1:T(8,128)(2,1)}, bf16[224,384]{0,1:T(8,128)(2,1)}, u32[]{:S(2)}, u32[]{:S(2)}) collective-permute-start(bf16[224,384]{0,1:T(8,128)(2,1)} %copy.128), channel_id=1, source_target_pairs={{16,0},{24,8},{32,16},{40,24},{48,32},{56,40},{64,48},{72,56},{80,... | collective-permute-start | bytes 516104 | tf_op jit(solution)/shard_map/ppermute | solution.py:20
  176.1 12.4 %copy-start.7 = (bf16[224,384]{0,1:T(8,128)(2,1)}, bf16[224,384]{0,1:T(8,128)(2,1)S(1)}, u32[]{:S(2)}) copy-start(bf16[224,384]{0,1:T(8,128)(2,1)S(1)} %collective-permute-done.8) | copy-start | bytes 516100
  176.1 23.7 %collective-permute-start.13 = (bf16[224,384]{0,1:T(8,128)(2,1)S(1)}, bf16[224,384]{0,1:T(8,128)(2,1)}, u32[]{:S(2)}, u32[]{:S(2)}) collective-permute-start(bf16[224,384]{0,1:T(8,128)(2,1)S(1)} %copy.133), channel_id=1, source_target_pairs={{16,0},{24,8},{32,16},{40,24},{48,32},{56,40},{64,48},{72,56},{80,... | collective-permute-start | bytes 516104 | tf_op jit(solution)/shard_map/ppermute | solution.py:20
  180.3 3.1 %copy-start.3 = (bf16[224,384]{0,1:T(8,128)(2,1)}, bf16[224,384]{0,1:T(8,128)(2,1)S(1)}, u32[]{:S(2)}) copy-start(bf16[224,384]{0,1:T(8,128)(2,1)S(1)} %collective-permute-done.9) | copy-start | bytes 516100
  180.3 22.2 %collective-permute-start.14 = (bf16[224,384]{0,1:T(8,128)(2,1)}, bf16[224,384]{0,1:T(8,128)(2,1)}, u32[]{:S(2)}, u32[]{:S(2)}) collective-permute-start(bf16[224,384]{0,1:T(8,128)(2,1)} %copy.128), channel_id=1, source_target_pairs={{8,0},{16,8},{24,16},{32,24},{40,32},{48,40},{56,48},{64,56},{72,6... | collective-permute-start | bytes 516104 | tf_op jit(solution)/shard_map/ppermute | solution.py:20
  186.5 1.9 copy-start.6
  186.5 16.1 %collective-permute-start.15 = (bf16[224,384]{0,1:T(8,128)(2,1)S(1)}, bf16[224,384]{0,1:T(8,128)(2,1)S(1)}, u32[]{:S(2)}, u32[]{:S(2)}) collective-permute-start(bf16[224,384]{0,1:T(8,128)(2,1)S(1)} %copy.133), channel_id=1, source_target_pairs={{8,0},{16,8},{24,16},{32,24},{40,32},{48,40},{56,48},{64,56},{72,6... | collective-permute-start | bytes 516104 | tf_op jit(solution)/shard_map/ppermute | solution.py:20
  206.8 53.8 %copy-start.9 = (bf16[224,384]{1,0:T(8,128)(2,1)S(1)}, bf16[224,384]{1,0:T(8,128)(2,1)}, u32[]{:S(2)}) copy-start(bf16[224,384]{1,0:T(8,128)(2,1)} %param.36) | copy-start | bytes 516100
  206.8 53.8 %copy-start.10 = (f32[384]{0:T(512)S(1)}, f32[384]{0:T(512)}, u32[]{:S(2)}) copy-start(f32[384]{0:T(512)} %param.37) | copy-start | bytes 4612
Sparse Core Ops, SparseCore 0:
  33.5 117.8 all-reduce.2
  209.5 49.9 reduce-scatter.3
where the time goes:
time: 271 us; the launch traced here: 268 us
  waiting for transfers between devices  165 us (61%)
  starting transfers between devices  40.3 us (15%)
  matrix products  21.9 us (8%)
  between operations  20.1 us (7%)
  local copies, waits for them, and re-layouts  15.5 us (6%)
  other arithmetic  5.24 us (2%)
    psum x1, waiting for transfers between devices, broadcast(): return lax.psum(block, axis)  108 us
    unnamed x3, waiting for transfers between devices  50.2 us
    ppermute x16, starting transfers between devices, from_behind(): return lax.ppermute(block, axis, route)  40.3 us
    unnamed x35, local copies, waits for them, and re-layouts  11.9 us
    dot_general x8, matrix products, absorb(): jnp.einsum('qhd,khd->hqk', query_heads, key_heads, preferred_element_type...  11.4 us
    dot_general x8, matrix products, absorb(): jnp.einsum('hqk,khd->qhd', weights.astype(jnp.bfloat16), value_heads, pre...  8.54 us
    ppermute x16, waiting for transfers between devices, from_behind(): return lax.ppermute(block, axis, route)  7.11 us
  transfers between devices with their start and end apart: 18, of which 5 were waited for; matrix products, arithmetic and copies ran while one was open for 12% of the time, Pallas kernels for 0%

commit v1 on v0

v1 whole, which is shorter than its diff:
```python
import math

import jax
import jax.numpy as jnp
from jax import lax
from jax.experimental import pallas as pl
from jax.experimental.pallas import tpu as pltpu
from jax.sharding import PartitionSpec as P

HD = 128
REACH = 4
MESH = pl.DeviceIdType.MESH
SCALE = math.log2(math.e) / math.sqrt(HD)
FAR = 1e30
LANES = 128


def dot(a, b, dims):
    return lax.dot_general(a, b, (dims, ((), ())), preferred_element_type=jnp.float32)


def kernel(
    q_hbm, k_hbm, v_hbm, rk_hbm, rv_hbm, lists, counts, owner, w_hbm, res_hbm, gate_ref,
    out_ref,
    q_buf, k_near, v_near, ref_own, ref_sib, ref_sel, x_parts, x_sum, y_parts, style,
    w_buf, res_buf, top, total, acc, att, z_out, z_in, local_sem, send_sem, recv_sem, z_send, z_recv,
):
    rows, width = q_buf.shape
    heads = width // HD
    slots = lists.shape[1]
    ref_rows = style.shape[1]
    quarter, piece = ref_rows // 4, ref_rows // 16
    half = rows // 2

    frame = lax.axis_index("frame")
    z = lax.axis_index("head")
    core = lax.rem(frame, 2)
    chip = frame // 2
    x, y = chip // 4, lax.rem(chip, 4)
    sibling = (frame + 1 - 2 * core, z)

    def at_x(j):
        return (lax.rem(x + j, 4) * 8 + y * 2 + core, z)

    def at_y(j):
        return (x * 8 + lax.rem(y + j, 4) * 2 + core, z)

    def at_chip(o):
        return (lax.rem(chip + o + 16, 16) * 2 + core, z)

    def at_z(o):
        return (frame, lax.rem(z + o + 8, 8))

    made = []

    def send(src, dst, device):
        i = len(made)
        copy = pltpu.make_async_remote_copy(
            src_ref=src, dst_ref=dst, send_sem=send_sem.at[i], recv_sem=recv_sem.at[i],
            device_id=device, device_id_type=MESH,
        )
        copy.start()
        made.append(copy)
        return copy

    def fetch(src, dst, i):
        copy = pltpu.make_async_copy(src, dst, local_sem.at[i])
        copy.start()
        return copy

    own = 4 + core
    get_q = fetch(q_hbm, q_buf, 0)
    get_k = fetch(k_hbm, k_near.at[own], 1)
    get_v = fetch(v_hbm, v_near.at[own], 2)

    @pl.when(core == 0)
    def _():
        pltpu.make_async_copy(rk_hbm.at[0], ref_own, local_sem.at[3]).start()

    @pl.when(core == 1)
    def _():
        pltpu.make_async_copy(rv_hbm.at[0], ref_own, local_sem.at[3]).start()

    get_w = fetch(w_hbm, w_buf, 4)
    get_res = fetch(res_hbm, res_buf, 5)

    barrier = pltpu.get_barrier_semaphore()
    partners = (
        [sibling]
        + [at_x(j) for j in (1, 2, 3)]
        + [at_y(j) for j in (1, 2, 3)]
        + [at_chip(o) for o in (1, -1, 2, -2)]
        + [at_z(1), at_z(-1)]
    )
    for device in partners:
        pl.semaphore_signal(barrier, inc=1, device_id=device, device_id_type=MESH)
    pl.semaphore_wait(barrier, len(partners))

    swap = pltpu.make_async_remote_copy(
        src_ref=rv_hbm.at[0], dst_ref=ref_sib, send_sem=send_sem.at[0], recv_sem=recv_sem.at[0],
        device_id=sibling, device_id_type=MESH,
    )
    made.append(swap)
    pl.when(core == 0)(swap.start)

    @pl.when(core == 1)
    def _():
        pltpu.make_async_remote_copy(
            src_ref=rk_hbm.at[0], dst_ref=ref_sib, send_sem=send_sem.at[0], recv_sem=recv_sem.at[0],
            device_id=sibling, device_id_type=MESH,
        ).start()

    to_sib = [send(k_hbm, k_near.at[own], sibling), send(v_hbm, v_near.at[own], sibling)]

    def to_chip(o):
        slot = (2 - o) * 2 + core
        return [send(k_hbm, k_near.at[slot], at_chip(o)), send(v_hbm, v_near.at[slot], at_chip(o))]

    near = {o: to_chip(o) for o in (1, -1)}

    top[...] = jnp.full(top.shape, -FAR, jnp.float32)
    total[...] = jnp.zeros(total.shape, jnp.float32)
    acc[...] = jnp.zeros(acc.shape, jnp.float32)

    def absorb(k_ref, v_ref, penalty):
        for h in range(heads):
            cols = pl.ds(h * HD, HD)
            scores = dot(k_ref[:, cols], q_buf[:, cols], ((1,), (1,)))
            best = jnp.max(scores, axis=0, keepdims=True)
            if penalty is not None:
                best = best - penalty
            before = top[h]
            after = jnp.maximum(before, best)
            factor = jnp.exp2((before - after) * SCALE)
            shift = after * SCALE
            if penalty is not None:
                shift = shift + penalty
            weights = jnp.exp2(scores * SCALE - shift)
            top[h] = after
            total[h] = total[h] * factor + jnp.sum(weights, axis=0, keepdims=True)
            acc[h] = acc[h] * factor + dot(v_ref[:, cols], weights.astype(jnp.bfloat16), ((0,), (0,)))

    def absorb_near(slot):
        there = frame - core - 4 + slot
        hits = jnp.int32(0)
        for j in range(slots):
            hits += jnp.where((lists[0, j] == there) & (j < counts[0]), 1, 0)
        penalty = jnp.where(hits > 0, jnp.float32(0), jnp.float32(FAR))
        absorb(k_near.at[slot], v_near.at[slot], penalty)

    def absorb_two(slot_a, slot_b):
        def body(i, carry):
            absorb_near(slot_a + i * (slot_b - slot_a))
            return carry

        lax.fori_loop(0, 2, body, 0)

    get_q.wait()
    get_k.wait()
    get_v.wait()
    absorb(k_near.at[own], v_near.at[own], None)

    pltpu.make_async_copy(rk_hbm.at[0], ref_own, local_sem.at[3]).wait()
    swap.wait_recv()
    mine = jnp.where(owner[0] == frame, 1.0, 0.0).astype(jnp.bfloat16)
    theirs = jnp.where(owner[0] == frame + 1 - 2 * core, 1.0, 0.0).astype(jnp.bfloat16)
    ref_sel[...] = ref_own[...] * mine + ref_sib[...] * theirs

    def q_rows(j):
        return pl.ds(pl.multiple_of(lax.rem(x + j, 4) * quarter, quarter), quarter)

    rsx = [send(ref_sel.at[q_rows(j)], x_parts.at[j - 1], at_x(j)) for j in (1, 3, 2)]
    near.update({o: to_chip(o) for o in (2, -2)})

    for copy in to_sib:
        copy.wait_recv()
    absorb_near(5 - core)

    passed = []

    def pass_on(slot):
        return [send(k_near.at[slot], k_near.at[slot], sibling), send(v_near.at[slot], v_near.at[slot], sibling)]

    for o in (1, -1):
        for copy in near[o]:
            copy.wait_recv()
        passed += pass_on((2 - o) * 2 + core)
    absorb_two(2 + core, 6 + core)

    for copy in rsx:
        copy.wait_recv()
    x_sum[...] = ref_sel[q_rows(0)] + x_parts[0] + x_parts[1] + x_parts[2]

    def p_rows(j):
        return pl.ds(pl.multiple_of(lax.rem(y + j, 4) * piece, piece), piece)

    rsy = [send(x_sum.at[p_rows(j)], y_parts.at[j - 1], at_y(j)) for j in (1, 3, 2)]

    for copy in passed:
        copy.wait_recv()
    absorb_two(3 - core, 7 - core)

    for copy in rsy:
        copy.wait_recv()
    my_piece = pl.ds(pl.multiple_of(x * quarter + y * piece, piece), piece)
    carried = style.at[core]
    carried[my_piece] = x_sum[p_rows(0)] + y_parts[0] + y_parts[1] + y_parts[2]
    agy = [send(carried.at[my_piece], carried.at[my_piece], at_y(j)) for j in (1, 3, 2)]

    for o in (2, -2):
        for copy in near[o]:
            copy.wait_recv()
    last = pass_on(8 - 7 * core)
    absorb_two(core, 8 + core)

    for copy in agy:
        copy.wait_recv()
    agx = {j: send(carried.at[q_rows(0)], carried.at[q_rows(0)], at_x(j)) for j in (1, 3, 2)}
    shown = send(carried.at[q_rows(0)], carried.at[q_rows(0)], sibling)

    for copy in last:
        copy.wait_recv()
    absorb_near(1 + 7 * core)

    shown.wait_recv()

    def absorb_style(j):
        absorb(style.at[0, q_rows(j)], style.at[1, q_rows(j)], None)

    absorb_style(0)
    for j in (1, 3, 2):
        agx[j].wait_recv()
        there = q_rows(4 - j)
        shown = send(carried.at[there], carried.at[there], sibling)
        shown.wait_recv()
        absorb_style(4 - j)

    for h in range(heads):
        att[:, pl.ds(h * HD, HD)] = (acc[h] / total[h]).T.astype(jnp.bfloat16)

    get_w.wait()
    parts = width // LANES

    def share(way, step):
        chunk = lax.rem(z - 1 - step + 16, 8) if way == 0 else lax.rem(z + 1 + step, 8)
        cols = pl.ds(pl.multiple_of(chunk * width, LANES), width)
        return dot(att[pl.ds(way * half, half), :], w_buf[:, cols], ((1,), (0,)))

    def hop(way, step, part):
        i = (step * 2 + way) * parts + part
        return pltpu.make_async_remote_copy(
            src_ref=z_out.at[step, way, part], dst_ref=z_in.at[step, way, part],
            send_sem=z_send.at[i], recv_sem=z_recv.at[i],
            device_id=at_z(1 if way == 0 else -1), device_id_type=MESH,
        )

    def ring(step, first):
        shares = [share(way, step) for way in (0, 1)]
        for part in range(parts):
            for way in (0, 1):
                value = shares[way][:, part * LANES : (part + 1) * LANES]
                if not first:
                    hop(way, step - 1, part).wait_recv()
                    value = value + z_in[step - 1, way, part].astype(jnp.float32)
                z_out[step, way, part] = value.astype(jnp.bfloat16)
                hop(way, step, part).start()

    ring(0, True)

    def body(step, carry):
        ring(step, False)
        return carry

    lax.fori_loop(1, 7, body, 0)
    get_res.wait()
    shares = [share(way, 7) for way in (0, 1)]
    for part in range(parts):
        for way in (0, 1):
            hop(way, 6, part).wait_recv()
            cols = pl.ds(part * LANES, LANES)
            some = pl.ds(way * half, half)
            value = shares[way][:, part * LANES : (part + 1) * LANES] + z_in[6, way, part].astype(jnp.float32)
            out_ref[some, cols] = (
                res_buf[some, cols].astype(jnp.float32) + gate_ref[:, cols] * value
            ).astype(jnp.bfloat16)

    for copy in made:
        copy.wait_send()

    def drain(step, carry):
        for way in (0, 1):
            for part in range(parts):
                hop(way, step, part).wait_send()
        return carry

    lax.fori_loop(0, 7, drain, 0)


def per_device(
    queries, key_rows, value_rows, ref_keys, ref_values, key_lists, list_counts, owner_index, out_weight, residual,
    gate_scale,
):
    rows, width = queries.shape
    heads = width // HD
    ref_rows = ref_keys.shape[1]
    quarter, piece = ref_rows // 4, ref_rows // 16
    bf16, f32 = jnp.bfloat16, jnp.float32
    hbm = pl.BlockSpec(memory_space=pl.ANY)
    vmem = pl.BlockSpec(memory_space=pltpu.VMEM)
    smem = pl.BlockSpec(memory_space=pltpu.SMEM)
    copies = 40
    hops = 7 * 2 * (width // LANES)
    return pl.pallas_call(
        kernel,
        out_shape=jax.ShapeDtypeStruct((rows, width), bf16),
        in_specs=[hbm] * 5 + [smem] * 3 + [hbm, hbm, vmem],
        out_specs=vmem,
        scratch_shapes=[
            pltpu.VMEM((rows, width), bf16),
            pltpu.VMEM((10, rows, width), bf16),
            pltpu.VMEM((10, rows, width), bf16),
            pltpu.VMEM((ref_rows, width), bf16),
            pltpu.VMEM((ref_rows, width), bf16),
            pltpu.VMEM((ref_rows, width), bf16),
            pltpu.VMEM((3, quarter, width), bf16),
            pltpu.VMEM((quarter, width), bf16),
            pltpu.VMEM((3, piece, width), bf16),
            pltpu.VMEM((2, ref_rows, width), bf16),
            pltpu.VMEM(out_weight.shape, bf16),
            pltpu.VMEM((rows, width), bf16),
            pltpu.VMEM((heads, 1, rows), f32),
            pltpu.VMEM((heads, 1, rows), f32),
            pltpu.VMEM((heads, HD, rows), f32),
            pltpu.VMEM((rows, width), bf16),
            pltpu.VMEM((7, 2, width // LANES, rows // 2, LANES), bf16),
            pltpu.VMEM((7, 2, width // LANES, rows // 2, LANES), bf16),
            pltpu.SemaphoreType.DMA((6,)),
            pltpu.SemaphoreType.DMA((copies,)),
            pltpu.SemaphoreType.DMA((copies,)),
            pltpu.SemaphoreType.DMA((hops,)),
            pltpu.SemaphoreType.DMA((hops,)),
        ],
        compiler_params=pltpu.CompilerParams(
            collective_id=0, has_side_effects=True, vmem_limit_bytes=48 * 1024 * 1024
        ),
        name="block",
    )(
        queries, key_rows, value_rows, ref_keys, ref_values, key_lists, list_counts, owner_index, out_weight,
        residual, gate_scale.reshape(1, width),
    )


def solution(mesh):
    placed = (
        P("frame", "head"),
        P("frame", "head"),
        P("frame", "head"),
        P("frame", None, "head"),
        P("frame", None, "head"),
        P("frame", None),
        P("frame"),
        P(),
        P("head", None),
        P("frame", "head"),
        P("head"),
    )
    return jax.shard_map(
        per_device, mesh=mesh, in_specs=placed, out_specs=P("frame", "head"), check_vma=False
    )
```

time: 271 us -> 94.3 us (0.35)
  waiting for transfers between devices: 165 us -> 0 us
  Pallas kernels: 0 us -> 83 us
  starting transfers between devices: 40.3 us -> 0 us
  matrix products: 21.9 us -> 0 us
  between operations: 20.1 us -> 1.31 us
  local copies, waits for them, and re-layouts: 15.5 us -> 9.61 us
  other arithmetic: 5.24 us -> 0 us
    psum x1 -> x0, waiting for transfers between devices: 108 us -> none  [broadcast(): return lax.psum(block, axis)]
    pallas_call x0 -> x1, Pallas kernels: none -> 83 us  [per_device(): pl.pallas_call(kernel, out_shape=jax.ShapeDtypeStruct((rows, width), bf16...]
    unnamed x3 -> x0, waiting for transfers between devices: 50.2 us -> none
    ppermute x16 -> x0, starting transfers between devices: 40.3 us -> none  [from_behind(): return lax.ppermute(block, axis, route)]
    dot_general x17 -> x0, matrix products: 21.9 us -> none  [the longest x8 11.4 us: absorb(): jnp.einsum('qhd,khd->hqk', query_heads, key_heads, preferred_element_type...]
    ppermute x16 -> x0, waiting for transfers between devices: 7.11 us -> none  [from_behind(): return lax.ppermute(block, axis, route)]
    another operation x2 -> x0, local copies, waits for them, and re-layouts: 3.45 us -> none  [the longest x1 2.28 us: absorb(): key_heads = key_block.reshape(key_block.shape[0], head_count, HD)]
    unnamed x35 -> x17, local copies, waits for them, and re-layouts: 11.9 us -> 8.93 us
  transfers between devices with their start and end apart: 18 -> 0, of which waited for: 5 -> 0; matrix products, arithmetic and copies ran while one was open for 12% -> 0% of each run, Pallas kernels for 0% -> 0%
where the time goes in v1:
time: 94.3 us; the launch traced here: 93.9 us
  Pallas kernels  83 us (88%)
  local copies, waits for them, and re-layouts  9.61 us (10%)
  between operations  1.31 us (1%)
    pallas_call x1, Pallas kernels, per_device(): pl.pallas_call(kernel, out_shape=jax.ShapeDtypeStruct((rows, width), bf16...  83 us
    unnamed x17, local copies, waits for them, and re-layouts  8.93 us

profile of v1, /device:TPU:8, one launch (start us, length us, event | category | flops | bytes accessed | tf_op | source)
XLA Modules:
  0.0 93.9 jit_solution(11088880662257430525)
XLA Ops:
  1.3 0.7 reshape.3.gate_ref
  2.0 0.0 copy-start
  2.0 1.7 %copy-done = bf16[384,3072]{1,0:T(8,128)(2,1)S(1)} copy-done((bf16[384,3072]{1,0:T(8,128)(2,1)S(1)}, bf16[384,3072]{1,0:T(8,128)(2,1)}, u32[]{:S(2)}) %copy-start) | copy-done | bytes 2359320
  3.6 0.0 copy-start.1
  3.6 1.1 %copy-done.1 = bf16[1,1024,384]{2,1,0:T(8,128)(2,1)S(1)} copy-done((bf16[1,1024,384]{2,1,0:T(8,128)(2,1)S(1)}, bf16[1,1024,384]{2,1,0:T(8,128)(2,1)}, u32[]{:S(2)}) %copy-start.1) | copy-done | bytes 786456
  4.8 0.0 copy-start.2
  4.8 1.1 %copy-done.2 = bf16[1,1024,384]{2,1,0:T(8,128)(2,1)S(1)} copy-done((bf16[1,1024,384]{2,1,0:T(8,128)(2,1)S(1)}, bf16[1,1024,384]{2,1,0:T(8,128)(2,1)}, u32[]{:S(2)}) %copy-start.2) | copy-done | bytes 786456
  5.9 0.0 copy-start.3
  5.9 0.9 copy-done.3
  6.8 0.0 copy-start.4
  6.8 0.9 copy-done.4
  7.8 0.0 copy-start.5
  7.8 0.9 copy-done.5
  8.7 0.0 copy-start.6
  8.7 0.9 copy-done.6
  9.6 0.0 copy-start.7
  9.6 0.7 copy-done.7
  10.2 83.0 %block.1 = bf16[224,384]{1,0:T(8,128)(2,1)S(1)} custom-call(bf16[224,384]{1,0:T(8,128)(2,1)S(1)} %copy-done.3, bf16[224,384]{1,0:T(8,128)(2,1)S(1)} %copy-done.4, bf16[224,384]{1,0:T(8,128)(2,1)S(1)} %copy-done.5, bf16[1,1024,384]{2,1,0:T(8,128)(2,1)S(1)} %copy-done.1, bf16[1,1024,384]{2,1,0:T(8,128)(2,1)S(1)} %copy-done.2, s32[1,8]{1,0:T(1,128)S(1)} %copy-done.7, ...), custom_call_target="tpu_custom_call" | custom-call | tf_op jit(solution)/shard_map/block/pallas_call | solution.py:313
  93.3 0.7 copy.15
Async XLA Ops:
  2.0 1.7 %copy-start = (bf16[384,3072]{1,0:T(8,128)(2,1)S(1)}, bf16[384,3072]{1,0:T(8,128)(2,1)}, u32[]{:S(2)}) copy-start(bf16[384,3072]{1,0:T(8,128)(2,1)} %w_hbm.1) | copy-start | bytes 7077892
  3.6 1.1 %copy-start.1 = (bf16[1,1024,384]{2,1,0:T(8,128)(2,1)S(1)}, bf16[1,1024,384]{2,1,0:T(8,128)(2,1)}, u32[]{:S(2)}) copy-start(bf16[1,1024,384]{2,1,0:T(8,128)(2,1)} %rk_hbm.1) | copy-start | bytes 2359300
  4.8 1.1 %copy-start.2 = (bf16[1,1024,384]{2,1,0:T(8,128)(2,1)S(1)}, bf16[1,1024,384]{2,1,0:T(8,128)(2,1)}, u32[]{:S(2)}) copy-start(bf16[1,1024,384]{2,1,0:T(8,128)(2,1)} %rv_hbm.1) | copy-start | bytes 2359300
  5.9 0.9 copy-start.3
  6.8 0.9 copy-start.4
  7.8 0.9 copy-start.5
  8.7 0.9 copy-start.6
  9.6 0.7 copy-start.7

commit v2 on v1

v2 whole, which is shorter than its diff:
```python
import math

import jax
import jax.numpy as jnp
from jax import lax
from jax.experimental import pallas as pl
from jax.experimental.pallas import tpu as pltpu
from jax.sharding import PartitionSpec as P

HD = 128
REACH = 4
MESH = pl.DeviceIdType.MESH
SCALE = math.log2(math.e) / math.sqrt(HD)
FAR = 1e30
LANES = 128


def dot(a, b, dims):
    return lax.dot_general(a, b, (dims, ((), ())), preferred_element_type=jnp.float32)


def kernel(
    q_hbm, k_hbm, v_hbm, rk_hbm, rv_hbm, lists, counts, owner, w_hbm, res_hbm, gate_ref,
    out_ref,
    q_buf, k_near, v_near, ref_own, ref_sib, ref_sel, x_parts, x_sum, y_parts, style,
    w_buf, res_buf, top, total, acc, att, z_out, z_in, local_sem, send_sem, recv_sem, z_send, z_recv,
):
    rows, width = q_buf.shape
    heads = width // HD
    slots = lists.shape[1]
    ref_rows = style.shape[1]
    half = rows // 2

    frame = lax.axis_index("frame")
    z = lax.axis_index("head")
    core = lax.rem(frame, 2)
    chip = frame // 2
    x, y = chip // 4, lax.rem(chip, 4)
    sibling = (frame + 1 - 2 * core, z)

    def at_x(j):
        return (lax.rem(x + j, 4) * 8 + y * 2 + core, z)

    def at_y(j):
        return (x * 8 + lax.rem(y + j, 4) * 2 + core, z)

    def at_chip(o):
        return (lax.rem(chip + o + 16, 16) * 2 + core, z)

    def at_z(o):
        return (frame, lax.rem(z + o + 8, 8))

    made = []

    def send(src, dst, device):
        i = len(made)
        copy = pltpu.make_async_remote_copy(
            src_ref=src, dst_ref=dst, send_sem=send_sem.at[i], recv_sem=recv_sem.at[i],
            device_id=device, device_id_type=MESH,
        )
        copy.start()
        made.append(copy)
        return copy

    def fetch(src, dst, i):
        copy = pltpu.make_async_copy(src, dst, local_sem.at[i])
        copy.start()
        return copy

    own = 4 + core
    block, bit = ref_rows // 8, ref_rows // 32
    get_q = fetch(q_hbm, q_buf, 0)
    get_k = fetch(k_hbm, k_near.at[own], 1)
    get_v = fetch(v_hbm, v_near.at[own], 2)

    style_in = ((rk_hbm, rv_hbm), (rv_hbm, rk_hbm))

    def keep(s, which):
        rows_of = pl.ds(s * 4 * block, 4 * block)
        return pltpu.make_async_copy(style_in[which][0].at[0, rows_of], ref_own.at[rows_of], local_sem.at[3 + s])

    def give(s, which):
        rows_of = pl.ds(s * 4 * block, 4 * block)
        return pltpu.make_async_remote_copy(
            src_ref=style_in[which][1].at[0, rows_of], dst_ref=ref_sib.at[rows_of],
            send_sem=send_sem.at[s], recv_sem=recv_sem.at[s], device_id=sibling, device_id_type=MESH,
        )

    for which in (0, 1):

        @pl.when(core == which)
        def _():
            for s in (0, 1):
                keep(s, which).start()

    get_w = fetch(w_hbm, w_buf, 5)
    get_res = fetch(res_hbm, res_buf, 6)

    barrier = pltpu.get_barrier_semaphore()
    partners = (
        [sibling]
        + [at_x(j) for j in (1, 2, 3)]
        + [at_y(j) for j in (1, 2, 3)]
        + [at_chip(o) for o in (1, -1)]
        + [at_z(1), at_z(-1)]
    )
    for device in partners:
        pl.semaphore_signal(barrier, inc=1, device_id=device, device_id_type=MESH)
    pl.semaphore_wait(barrier, len(partners))

    for which in (0, 1):

        @pl.when(core == which)
        def _():
            for s in (0, 1):
                give(s, which).start()

    made += [give(s, 0) for s in (0, 1)]

    to_sib = [send(k_hbm, k_near.at[own], sibling), send(v_hbm, v_near.at[own], sibling)]

    def slot_of(o):
        return (o + 2) * 2 + core

    near = {(o, 0): send(k_hbm, k_near.at[slot_of(-o)], at_chip(o)) for o in (1, -1)}

    top[...] = jnp.full(top.shape, -FAR, jnp.float32)
    total[...] = jnp.zeros(total.shape, jnp.float32)
    acc[...] = jnp.zeros(acc.shape, jnp.float32)

    def absorb(k_ref, v_ref, penalty):
        for h in range(heads):
            cols = pl.ds(h * HD, HD)
            scores = dot(k_ref[:, cols], q_buf[:, cols], ((1,), (1,)))
            best = jnp.max(scores, axis=0, keepdims=True)
            if penalty is not None:
                best = best - penalty
            before = top[h]
            after = jnp.maximum(before, best)
            factor = jnp.exp2((before - after) * SCALE)
            shift = after * SCALE
            if penalty is not None:
                shift = shift + penalty
            weights = jnp.exp2(scores * SCALE - shift)
            top[h] = after
            total[h] = total[h] * factor + jnp.sum(weights, axis=0, keepdims=True)
            acc[h] = acc[h] * factor + dot(v_ref[:, cols], weights.astype(jnp.bfloat16), ((0,), (0,)))

    def absorb_near(slot):
        there = frame - core - 4 + slot
        hits = jnp.int32(0)
        for j in range(slots):
            hits += jnp.where((lists[0, j] == there) & (j < counts[0]), 1, 0)
        penalty = jnp.where(hits > 0, jnp.float32(0), jnp.float32(FAR))
        absorb(k_near.at[slot], v_near.at[slot], penalty)

    def absorb_two(slot_a, slot_b):
        def body(i, carry):
            absorb_near(slot_a + i * (slot_b - slot_a))
            return carry

        lax.fori_loop(0, 2, body, 0)

    first_axis, first_at, second_axis, second_at = (x, y), (at_x, at_y), (y, x), (at_y, at_x)
    order = (1, 3, 2)
    mine = jnp.where(owner[0] == frame, 1.0, 0.0).astype(jnp.bfloat16)
    theirs = jnp.where(owner[0] == frame + 1 - 2 * core, 1.0, 0.0).astype(jnp.bfloat16)
    carried = style.at[core]

    def block_rows(s, j):
        return pl.ds(pl.multiple_of(s * 4 * block + lax.rem(first_axis[s] + j, 4) * block, block), block)

    def bit_rows(s, j):
        return pl.ds(pl.multiple_of(lax.rem(second_axis[s] + j, 4) * bit, bit), bit)

    def own_bit(s):
        return pl.ds(
            pl.multiple_of(s * 4 * block + first_axis[s] * block + second_axis[s] * bit, bit), bit
        )

    def choose(s):
        rows_of = pl.ds(s * 4 * block, 4 * block)
        keep(s, 0).wait()
        made[s].wait_recv()
        ref_sel[rows_of] = ref_own[rows_of] * mine + ref_sib[rows_of] * theirs
        return [send(ref_sel.at[block_rows(s, j)], x_parts.at[s, j - 1], first_at[s](j)) for j in order]

    def narrow(s, copies):
        for copy in copies:
            copy.wait_recv()
        x_sum[s] = ref_sel[block_rows(s, 0)] + x_parts[s, 0] + x_parts[s, 1] + x_parts[s, 2]
        return [send(x_sum.at[s, bit_rows(s, j)], y_parts.at[s, j - 1], second_at[s](j)) for j in order]

    def settle(s, copies):
        for copy in copies:
            copy.wait_recv()
        carried[own_bit(s)] = x_sum[s, bit_rows(s, 0)] + y_parts[s, 0] + y_parts[s, 1] + y_parts[s, 2]
        return [send(carried.at[own_bit(s)], carried.at[own_bit(s)], second_at[s](j)) for j in order]

    def widen(s, copies):
        for copy in copies:
            copy.wait_recv()
        here = carried.at[block_rows(s, 0)]
        return {j: send(here, here, first_at[s](j)) for j in order}, send(here, here, sibling)

    chosen = [choose(0), choose(1)]
    near.update({(o, 1): send(v_hbm, v_near.at[slot_of(-o)], at_chip(o)) for o in (1, -1)})

    get_q.wait()
    get_k.wait()
    get_v.wait()
    absorb(k_near.at[own], v_near.at[own], None)
    for copy in to_sib:
        copy.wait_recv()
    absorb_near(5 - core)

    far, passed = {}, []
    for part, hold in ((0, k_near), (1, v_near)):
        for o in (1, -1):
            near[o, part].wait_recv()
            got = hold.at[slot_of(-o)]
            far[o, part] = send(got, hold.at[slot_of(-2 * o)], at_chip(o))
            passed.append(send(got, got, sibling))
    absorb_two(slot_of(-1), slot_of(1))

    narrowed = [narrow(s, chosen[s]) for s in (0, 1)]

    for copy in passed:
        copy.wait_recv()
    absorb_two(3 - core, 7 - core)

    settled = [settle(s, narrowed[s]) for s in (0, 1)]

    for copy in far.values():
        copy.wait_recv()
    gone = 8 - 7 * core
    last = [send(hold.at[gone], hold.at[gone], sibling) for hold in (k_near, v_near)]
    absorb_two(core, 8 + core)

    widened = [widen(s, settled[s]) for s in (0, 1)]

    for copy in last:
        copy.wait_recv()
    absorb_near(1 + 7 * core)

    def absorb_style(j):
        def body(s, carry):
            axis = jnp.where(s == 0, x, y)
            there = pl.ds(pl.multiple_of(s * 4 * block + lax.rem(axis + j, 4) * block, block), block)
            absorb(style.at[0, there], style.at[1, there], None)
            return carry

        lax.fori_loop(0, 2, body, 0)

    for s in (0, 1):
        widened[s][1].wait_recv()
    absorb_style(0)
    for j in order:
        shown = []
        for s in (0, 1):
            widened[s][0][j].wait_recv()
            there = carried.at[block_rows(s, 4 - j)]
            shown.append(send(there, there, sibling))
        for copy in shown:
            copy.wait_recv()
        absorb_style(4 - j)

    for h in range(heads):
        att[:, pl.ds(h * HD, HD)] = (acc[h] / total[h]).T.astype(jnp.bfloat16)

    get_w.wait()
    parts = width // LANES
    signs = (1, -1)

    def share(ahead, some):
        cols = pl.ds(pl.multiple_of(lax.rem(z + ahead + 8, 8) * width, LANES), width)
        return dot(att[some, :], w_buf[:, cols], ((1,), (0,)))

    def hop(way, step, part):
        i = (step * 2 + way) * parts + part
        some = pl.ds(way * half, half) if step == 0 else pl.ds(0, rows)
        return pltpu.make_async_remote_copy(
            src_ref=z_out.at[step, way, part, some], dst_ref=z_in.at[step, way, part, some],
            send_sem=z_send.at[i], recv_sem=z_recv.at[i],
            device_id=at_z(signs[way]), device_id_type=MESH,
        )

    whole = pl.ds(0, rows)
    for step in range(4):
        for way in (0, 1):
            some = pl.ds(way * half, half) if step == 0 else whole
            mine_here = share(signs[way] * (4 - step), some)
            for part in range(parts):
                value = mine_here[:, part * LANES : (part + 1) * LANES]
                if step == 0:
                    z_out[step, way, part, some] = value.astype(jnp.bfloat16)
                elif step == 1:
                    hop(way, 0, part).wait_recv()
                    for piece_of in (0, 1):
                        here = pl.ds(piece_of * half, half)
                        one = value[piece_of * half : (piece_of + 1) * half]
                        if piece_of == way:
                            one = one + z_in[0, way, part, here].astype(jnp.float32)
                        z_out[step, way, part, here] = one.astype(jnp.bfloat16)
                else:
                    hop(way, step - 1, part).wait_recv()
                    z_out[step, way, part] = (value + z_in[step - 1, way, part].astype(jnp.float32)).astype(
                        jnp.bfloat16
                    )
                hop(way, step, part).start()

    get_res.wait()
    mine_here = share(0, whole)
    for part in range(parts):
        cols = pl.ds(part * LANES, LANES)
        value = mine_here[:, part * LANES : (part + 1) * LANES]
        for way in (0, 1):
            hop(way, 3, part).wait_recv()
            value = value + z_in[3, way, part].astype(jnp.float32)
        out_ref[:, cols] = (res_buf[:, cols].astype(jnp.float32) + gate_ref[:, cols] * value).astype(jnp.bfloat16)

    for copy in made:
        copy.wait_send()
    for step in range(4):
        for way in (0, 1):
            for part in range(parts):
                hop(way, step, part).wait_send()


def per_device(
    queries, key_rows, value_rows, ref_keys, ref_values, key_lists, list_counts, owner_index, out_weight, residual,
    gate_scale,
):
    rows, width = queries.shape
    heads = width // HD
    ref_rows = ref_keys.shape[1]
    block, bit = ref_rows // 8, ref_rows // 32
    bf16, f32 = jnp.bfloat16, jnp.float32
    hbm = pl.BlockSpec(memory_space=pl.ANY)
    vmem = pl.BlockSpec(memory_space=pltpu.VMEM)
    smem = pl.BlockSpec(memory_space=pltpu.SMEM)
    copies = 64
    hops = 4 * 2 * (width // LANES)
    return pl.pallas_call(
        kernel,
        out_shape=jax.ShapeDtypeStruct((rows, width), bf16),
        in_specs=[hbm] * 5 + [smem] * 3 + [hbm, hbm, vmem],
        out_specs=vmem,
        scratch_shapes=[
            pltpu.VMEM((rows, width), bf16),
            pltpu.VMEM((10, rows, width), bf16),
            pltpu.VMEM((10, rows, width), bf16),
            pltpu.VMEM((ref_rows, width), bf16),
            pltpu.VMEM((ref_rows, width), bf16),
            pltpu.VMEM((ref_rows, width), bf16),
            pltpu.VMEM((2, 3, block, width), bf16),
            pltpu.VMEM((2, block, width), bf16),
            pltpu.VMEM((2, 3, bit, width), bf16),
            pltpu.VMEM((2, ref_rows, width), bf16),
            pltpu.VMEM(out_weight.shape, bf16),
            pltpu.VMEM((rows, width), bf16),
            pltpu.VMEM((heads, 1, rows), f32),
            pltpu.VMEM((heads, 1, rows), f32),
            pltpu.VMEM((heads, HD, rows), f32),
            pltpu.VMEM((rows, width), bf16),
            pltpu.VMEM((4, 2, width // LANES, rows, LANES), bf16),
            pltpu.VMEM((4, 2, width // LANES, rows, LANES), bf16),
            pltpu.SemaphoreType.DMA((7,)),
            pltpu.SemaphoreType.DMA((copies,)),
            pltpu.SemaphoreType.DMA((copies,)),
            pltpu.SemaphoreType.DMA((hops,)),
            pltpu.SemaphoreType.DMA((hops,)),
        ],
        compiler_params=pltpu.CompilerParams(
            collective_id=0, has_side_effects=True, vmem_limit_bytes=60 * 1024 * 1024
        ),
        name="block",
    )(
        queries, key_rows, value_rows, ref_keys, ref_values, key_lists, list_counts, owner_index, out_weight,
        residual, gate_scale.reshape(1, width),
    )


def solution(mesh):
    placed = (
        P("frame", "head"),
        P("frame", "head"),
        P("frame", "head"),
        P("frame", None, "head"),
        P("frame", None, "head"),
        P("frame", None),
        P("frame"),
        P(),
        P("head", None),
        P("frame", "head"),
        P("head"),
    )
    return jax.shard_map(
        per_device, mesh=mesh, in_specs=placed, out_specs=P("frame", "head"), check_vma=False
    )
```

time: 94.3 us -> 76.4 us (0.81)
  Pallas kernels: 83 us -> 71.8 us
  local copies, waits for them, and re-layouts: 9.61 us -> 2.85 us
    pallas_call x1, Pallas kernels: 83 us -> 71.8 us  [per_device(): pl.pallas_call(kernel, out_shape=jax.ShapeDtypeStruct((rows, width), bf16...]
    unnamed x17 -> x1, local copies, waits for them, and re-layouts: 8.93 us -> 1.61 us
where the time goes in v2:
time: 76.4 us; the launch traced here: 76 us
  Pallas kernels  71.8 us (94%)
  local copies, waits for them, and re-layouts  2.85 us (4%)
  between operations  1.31 us (2%)
    pallas_call x1, Pallas kernels, per_device(): pl.pallas_call(kernel, out_shape=jax.ShapeDtypeStruct((rows, width), bf16...  71.8 us
    unnamed x1, local copies, waits for them, and re-layouts  1.61 us

profile of v2, /device:TPU:8, one launch (start us, length us, event | category | flops | bytes accessed | tf_op | source)
XLA Modules:
  0.0 76.0 jit_solution(11698997496973957515)
XLA Ops:
  1.3 1.2 %reshape.3.gate_ref = f32[1,384]{1,0:T(1,128)} reshape(f32[384]{0:T(512)} %param.21) | data formatting | bytes 3072 | tf_op jit(solution)/shard_map/reshape | solution.py:380
  2.5 71.8 %block.1 = bf16[224,384]{1,0:T(8,128)(2,1)} custom-call(bf16[224,384]{1,0:T(8,128)(2,1)} %q_hbm.1, bf16[224,384]{1,0:T(8,128)(2,1)} %k_hbm.1, bf16[224,384]{1,0:T(8,128)(2,1)} %v_hbm.1, bf16[1,1024,384]{2,1,0:T(8,128)(2,1)} %rk_hbm.1, bf16[1,1024,384]{2,1,0:T(8,128)(2,1)} %rv_hbm.1, s32[1,8]{1,0:T(1,128)} %lists.1, s32[1]{0:T(128)S(6)} %copy.13.counts, ...), custom_call_target="tpu_custom_call" | custom-call | tf_op jit(solution)/shard_map/block/pallas_call | solution.py:344
  74.4 1.6 %copy.15 = bf16[224,384]{1,0:T(8,128)(2,1)} copy(bf16[224,384]{1,0:T(8,128)(2,1)} %block.1) | data formatting | bytes 344064

commit v3 on v2

v3 whole, which is shorter than its diff:
```python
import math

import jax
import jax.numpy as jnp
from jax import lax
from jax.experimental import pallas as pl
from jax.experimental.pallas import tpu as pltpu
from jax.sharding import PartitionSpec as P

HD = 128
REACH = 4
MESH = pl.DeviceIdType.MESH
SCALE = math.log2(math.e) / math.sqrt(HD)
FAR = 1e30
LANES = 128


def dot(a, b, dims):
    return lax.dot_general(a, b, (dims, ((), ())), preferred_element_type=jnp.float32)


def kernel(
    q_hbm, k_hbm, v_hbm, rk_hbm, rv_hbm, lists, counts, owner, w_hbm,
    out_ref,
    q_buf, k_near, v_near, ref_own, ref_sib, ref_sel, x_parts, x_sum, y_parts, style,
    w_sum, w_all, top, total, acc, att, att_all, z_out, z_in, local_sem, send_sem, recv_sem, z_send, z_recv,
):
    rows, width = q_buf.shape
    slots = lists.shape[1]
    ref_rows = style.shape[1]
    half = rows // 2
    block, bit = ref_rows // 8, ref_rows // 32
    early = w_sum.shape[0]
    cols = (pl.ds(0, early), pl.ds(early, width - early))
    heads = (tuple(range(early // HD)), tuple(range(early // HD, width // HD)))
    late = width - early

    frame = lax.axis_index("frame")
    z = lax.axis_index("head")
    core = lax.rem(frame, 2)
    chip = frame // 2
    x, y = chip // 4, lax.rem(chip, 4)
    sibling = (frame + 1 - 2 * core, z)

    def at_x(j):
        return (lax.rem(x + j, 4) * 8 + y * 2 + core, z)

    def at_y(j):
        return (x * 8 + lax.rem(y + j, 4) * 2 + core, z)

    def at_chip(o):
        return (lax.rem(chip + o + 16, 16) * 2 + core, z)

    def ahead(o):
        return lax.rem(z + o + 8, 8)

    def at_z(o):
        return (frame, ahead(o))

    made = []

    def remote(src, dst, device):
        i = len(made)
        copy = pltpu.make_async_remote_copy(
            src_ref=src, dst_ref=dst, send_sem=send_sem.at[i], recv_sem=recv_sem.at[i],
            device_id=device, device_id_type=MESH,
        )
        made.append(copy)
        return copy

    def send(src, dst, device):
        copy = remote(src, dst, device)
        copy.start()
        return copy

    def fetch(src, dst, i):
        copy = pltpu.make_async_copy(src, dst, local_sem.at[i])
        copy.start()
        return copy

    own = 4 + core
    get_q = fetch(q_hbm, q_buf, 0)
    get_k = fetch(k_hbm, k_near.at[own], 1)
    get_v = fetch(v_hbm, v_near.at[own], 2)

    style_in = ((rk_hbm, rv_hbm), (rv_hbm, rk_hbm))

    def half_rows(s):
        return pl.ds(s * 4 * block, 4 * block)

    def keep(s, which):
        return pltpu.make_async_copy(
            style_in[which][0].at[0, half_rows(s)], ref_own.at[half_rows(s)], local_sem.at[3 + s]
        )

    def give(s, w, which, i):
        return pltpu.make_async_remote_copy(
            src_ref=style_in[which][1].at[0, half_rows(s), cols[w]], dst_ref=ref_sib.at[half_rows(s), cols[w]],
            send_sem=send_sem.at[i], recv_sem=recv_sem.at[i], device_id=sibling, device_id_type=MESH,
        )

    for which in (0, 1):

        @pl.when(core == which)
        def _():
            for s in (0, 1):
                keep(s, which).start()

    get_w = fetch(w_hbm.at[pl.ds(0, early)], w_sum, 5)

    def column_block(o):
        return pl.ds(pl.multiple_of(ahead(o) * width, LANES), width)

    get_own_w = fetch(w_hbm.at[pl.ds(early, late), column_block(0)], w_all.at[z], 6)

    barrier = pltpu.get_barrier_semaphore()
    partners = (
        [sibling]
        + [at_x(j) for j in (1, 2, 3)]
        + [at_y(j) for j in (1, 2, 3)]
        + [at_chip(o) for o in (1, -1)]
        + [at_z(o) for o in range(1, 8)]
    )
    for device in partners:
        pl.semaphore_signal(barrier, inc=1, device_id=device, device_id_type=MESH)
    pl.semaphore_wait(barrier, len(partners))

    gifts = [(s, w) for w in (0, 1) for s in (0, 1)]
    for which in (0, 1):

        @pl.when(core == which)
        def _():
            for i, (s, w) in enumerate(gifts):
                give(s, w, which, i).start()

    made += [give(s, w, 0, i) for i, (s, w) in enumerate(gifts)]
    given = {(s, w): made[i] for i, (s, w) in enumerate(gifts)}

    to_sib = [send(k_hbm, k_near.at[own], sibling), send(v_hbm, v_near.at[own], sibling)]

    def slot_of(o):
        return (o + 2) * 2 + core

    near, far, passed, gone = {}, {}, {}, {}

    def to_next(w, hbm, hold):
        for o in (1, -1):
            near[w, o, hbm is k_hbm] = send(hbm.at[:, cols[w]], hold.at[slot_of(-o), :, cols[w]], at_chip(o))

    def relay(w):
        passed[w], far[w] = [], []
        for hold in (k_near, v_near):
            for o in (1, -1):
                near[w, o, hold is k_near].wait_recv()
                got = hold.at[slot_of(-o), :, cols[w]]
                far[w].append(send(got, hold.at[slot_of(-2 * o), :, cols[w]], at_chip(o)))
                passed[w].append(send(got, got, sibling))

    def relay_far(w):
        for copy in far[w]:
            copy.wait_recv()
        slot = 8 - 7 * core
        gone[w] = [
            send(hold.at[slot, :, cols[w]], hold.at[slot, :, cols[w]], sibling) for hold in (k_near, v_near)
        ]

    to_next(0, k_hbm, k_near)
    w_moves = {
        o: send(w_hbm.at[pl.ds(early, late), column_block(o)], w_all.at[z], at_z(o)) for o in (4, 3, 5, 2, 6, 1, 7)
    }

    top[...] = jnp.full(top.shape, -FAR, jnp.float32)
    total[...] = jnp.zeros(total.shape, jnp.float32)
    acc[...] = jnp.zeros(acc.shape, jnp.float32)

    def absorb(w, blocks):
        for h in heads[w]:
            lanes = pl.ds(h * HD, HD)
            query = q_buf[:, lanes]
            scores = [dot(k_ref[:, lanes], query, ((1,), (1,))) for k_ref, _, _ in blocks]
            before = top[h]
            after = before
            for (_, _, penalty), score in zip(blocks, scores):
                best = jnp.max(score, axis=0, keepdims=True)
                after = jnp.maximum(after, best if penalty is None else best - penalty)
            factor = jnp.exp2((before - after) * SCALE)
            shift = after * SCALE
            weighted = acc[h] * factor
            sums = total[h] * factor
            for (_, v_ref, penalty), score in zip(blocks, scores):
                weights = jnp.exp2(score * SCALE - (shift if penalty is None else shift + penalty))
                sums = sums + jnp.sum(weights, axis=0, keepdims=True)
                weighted = weighted + dot(v_ref[:, lanes], weights.astype(jnp.bfloat16), ((0,), (0,)))
            top[h] = after
            total[h] = sums
            acc[h] = weighted

    def near_block(slot):
        there = frame - core - 4 + slot
        hits = jnp.int32(0)
        for j in range(slots):
            hits += jnp.where((lists[0, j] == there) & (j < counts[0]), 1, 0)
        penalty = jnp.where(hits > 0, jnp.float32(0), jnp.float32(FAR))
        return k_near.at[slot], v_near.at[slot], penalty

    def absorb_near(w, *which):
        absorb(w, [near_block(slot) for slot in which])

    first_axis, first_at, second_axis, second_at = (x, y), (at_x, at_y), (y, x), (at_y, at_x)
    order = (1, 3, 2)
    mine = jnp.where(owner[0] == frame, 1.0, 0.0).astype(jnp.bfloat16)
    theirs = jnp.where(owner[0] == frame + 1 - 2 * core, 1.0, 0.0).astype(jnp.bfloat16)
    carried = style.at[core]

    def block_rows(s, j):
        return pl.ds(pl.multiple_of(s * 4 * block + lax.rem(first_axis[s] + j, 4) * block, block), block)

    def bit_rows(s, j):
        return pl.ds(pl.multiple_of(lax.rem(second_axis[s] + j, 4) * bit, bit), bit)

    def own_bit(s):
        return pl.ds(
            pl.multiple_of(s * 4 * block + first_axis[s] * block + second_axis[s] * bit, bit), bit
        )

    chosen, narrowed, settled, widened, shown = {}, {}, {}, {}, {}

    def choose(s, w):
        c, r = cols[w], half_rows(s)
        if w == 0:
            keep(s, 0).wait()
        given[s, w].wait_recv()
        ref_sel[r, c] = ref_own[r, c] * mine + ref_sib[r, c] * theirs
        chosen[s, w] = [
            send(ref_sel.at[block_rows(s, j), c], x_parts.at[s, j - 1, :, c], first_at[s](j)) for j in order
        ]

    def narrow(s, w):
        c = cols[w]
        for copy in chosen[s, w]:
            copy.wait_recv()
        x_sum[s, :, c] = (
            ref_sel[block_rows(s, 0), c] + x_parts[s, 0, :, c] + x_parts[s, 1, :, c] + x_parts[s, 2, :, c]
        )
        narrowed[s, w] = [
            send(x_sum.at[s, bit_rows(s, j), c], y_parts.at[s, j - 1, :, c], second_at[s](j)) for j in order
        ]

    def settle(s, w):
        c = cols[w]
        for copy in narrowed[s, w]:
            copy.wait_recv()
        carried[own_bit(s), c] = (
            x_sum[s, bit_rows(s, 0), c] + y_parts[s, 0, :, c] + y_parts[s, 1, :, c] + y_parts[s, 2, :, c]
        )
        here = carried.at[own_bit(s), c]
        settled[s, w] = [send(here, here, second_at[s](j)) for j in order]

    def widen(s, w):
        for copy in settled[s, w]:
            copy.wait_recv()
        here = carried.at[block_rows(s, 0), cols[w]]
        widened[s, w] = {j: send(here, here, first_at[s](j)) for j in order}
        shown[s, w, 0] = send(here, here, sibling)

    def show(s, w, j):
        widened[s, w][j].wait_recv()
        there = carried.at[block_rows(s, 4 - j), cols[w]]
        shown[s, w, j] = send(there, there, sibling)

    def absorb_style(w, j):
        for s in (0, 1):
            shown[s, w, j].wait_recv()
        absorb(w, [(style.at[0, block_rows(s, 4 - j)], style.at[1, block_rows(s, 4 - j)], None) for s in (0, 1)])

    def both(stage, w):
        for s in (0, 1):
            stage(s, w)

    def finish(w):
        for h in heads[w]:
            att[:, pl.ds(h * HD, HD)] = (acc[h] / total[h]).T.astype(jnp.bfloat16)

    parts = width // LANES
    signs = (1, -1)
    whole = pl.ds(0, rows)

    def share(o, some):
        return dot(att[some, cols[0]], w_sum[:, column_block(o)], ((1,), (0,)))

    def hop(way, step, part):
        i = (step * 2 + way) * parts + part
        some = pl.ds(way * half, half) if step == 0 else whole
        return pltpu.make_async_remote_copy(
            src_ref=z_out.at[step, way, part, some], dst_ref=z_in.at[step, way, part, some],
            send_sem=z_send.at[i], recv_sem=z_recv.at[i],
            device_id=at_z(signs[way]), device_id_type=MESH,
        )

    def climb(step):
        for way in (0, 1):
            some = pl.ds(way * half, half) if step == 0 else whole
            here_share = share(signs[way] * (4 - step), some)
            for part in range(parts):
                value = here_share[:, part * LANES : (part + 1) * LANES]
                if step == 0:
                    z_out[step, way, part, some] = value.astype(jnp.bfloat16)
                elif step == 1:
                    hop(way, 0, part).wait_recv()
                    for which in (0, 1):
                        here = pl.ds(which * half, half)
                        one = value[which * half : (which + 1) * half]
                        if which == way:
                            one = one + z_in[0, way, part, here].astype(jnp.float32)
                        z_out[step, way, part, here] = one.astype(jnp.bfloat16)
                else:
                    hop(way, step - 1, part).wait_recv()
                    z_out[step, way, part] = (value + z_in[step - 1, way, part].astype(jnp.float32)).astype(
                        jnp.bfloat16
                    )
                hop(way, step, part).start()

    spread = {}

    def gather_near():
        mine_here = att.at[:, cols[1]]
        for o in (2, -2, 1, -1):
            spread[o] = send(mine_here, att_all.at[z], at_z(o))

    def gather_far():
        for way in (0, 1):
            o = signs[way]
            spread[2 * o].wait_recv()
            origin = ahead(-2 * o)
            some = pl.ds(way * half, half)
            spread[4 * o] = send(att_all.at[origin, some], att_all.at[origin, some], at_z(2 * o))
            spread[3 * o] = send(att_all.at[origin], att_all.at[origin], at_z(o))

    def late_share(o):
        return dot(att_all[ahead(o)], w_all[ahead(o)], ((1,), (0,)))

    both(choose, 0)
    to_next(0, v_hbm, v_near)
    get_q.wait()
    get_k.wait()
    get_v.wait()
    for copy in to_sib:
        copy.wait_recv()
    absorb(0, [(k_near.at[own], v_near.at[own], None), near_block(5 - core)])
    relay(0)
    to_next(1, k_hbm, k_near)
    to_next(1, v_hbm, v_near)
    both(choose, 1)
    absorb(1, [(k_near.at[own], v_near.at[own], None), near_block(5 - core)])
    both(narrow, 0)
    absorb_near(0, slot_of(-1), slot_of(1))
    both(settle, 0)
    both(narrow, 1)
    for copy in passed[0]:
        copy.wait_recv()
    absorb_near(0, 3 - core, 7 - core)
    both(widen, 0)
    both(settle, 1)
    relay_far(0)
    relay(1)
    absorb_near(0, slot_of(-2), slot_of(2))
    both(widen, 1)
    for copy in gone[0]:
        copy.wait_recv()
    absorb_near(0, 1 + 7 * core)
    absorb_style(0, 0)
    for j in order:
        for s in (0, 1):
            show(s, 0, j)
        absorb_style(0, j)
    finish(0)
    get_w.wait()
    climb(0)
    absorb_near(1, slot_of(-1), slot_of(1))
    for copy in passed[1]:
        copy.wait_recv()
    absorb_near(1, 3 - core, 7 - core)
    climb(1)
    relay_far(1)
    absorb_near(1, slot_of(-2), slot_of(2))
    absorb_style(1, 0)
    for j in order:
        for s in (0, 1):
            show(s, 1, j)
    climb(2)
    for copy in gone[1]:
        copy.wait_recv()
    absorb_near(1, 1 + 7 * core)
    for j in order:
        absorb_style(1, j)
    finish(1)
    gather_near()
    climb(3)
    att_all[z] = att[:, cols[1]]
    get_own_w.wait()
    for copy in w_moves.values():
        copy.wait_recv()
    out_ref[...] = share(0, whole) + late_share(0)
    gather_far()
    for o in (1, -1):
        spread[o].wait_recv()
    out_ref[...] += late_share(1) + late_share(-1) + late_share(2) + late_share(-2)
    for part in range(parts):
        lanes = pl.ds(part * LANES, LANES)
        for way in (0, 1):
            hop(way, 3, part).wait_recv()
        out_ref[:, lanes] += z_in[3, 0, part].astype(jnp.float32) + z_in[3, 1, part].astype(jnp.float32)
    for o in (3, -3, 4, -4):
        spread[o].wait_recv()
    out_ref[...] += late_share(3) + late_share(-3) + late_share(4)

    for copy in made:
        copy.wait_send()
    for step in range(4):
        for way in (0, 1):
            for part in range(parts):
                hop(way, step, part).wait_send()


def per_device(
    queries, key_rows, value_rows, ref_keys, ref_values, key_lists, list_counts, owner_index, out_weight, residual,
    gate_scale,
):
    rows, width = queries.shape
    heads = width // HD
    early = (heads - 1) * HD
    ref_rows = ref_keys.shape[1]
    block, bit = ref_rows // 8, ref_rows // 32
    bf16, f32 = jnp.bfloat16, jnp.float32
    hbm = pl.BlockSpec(memory_space=pl.ANY)
    vmem = pl.BlockSpec(memory_space=pltpu.VMEM)
    smem = pl.BlockSpec(memory_space=pltpu.SMEM)
    copies = 128
    hops = 4 * 2 * (width // LANES)
    projected = pl.pallas_call(
        kernel,
        out_shape=jax.ShapeDtypeStruct((rows, width), f32),
        in_specs=[hbm] * 5 + [smem] * 3 + [hbm],
        out_specs=vmem,
        scratch_shapes=[
            pltpu.VMEM((rows, width), bf16),
            pltpu.VMEM((10, rows, width), bf16),
            pltpu.VMEM((10, rows, width), bf16),
            pltpu.VMEM((ref_rows, width), bf16),
            pltpu.VMEM((ref_rows, width), bf16),
            pltpu.VMEM((ref_rows, width), bf16),
            pltpu.VMEM((2, 3, block, width), bf16),
            pltpu.VMEM((2, block, width), bf16),
            pltpu.VMEM((2, 3, bit, width), bf16),
            pltpu.VMEM((2, ref_rows, width), bf16),
            pltpu.VMEM((early, out_weight.shape[1]), bf16),
            pltpu.VMEM((8, width - early, width), bf16),
            pltpu.VMEM((heads, 1, rows), f32),
            pltpu.VMEM((heads, 1, rows), f32),
            pltpu.VMEM((heads, HD, rows), f32),
            pltpu.VMEM((rows, width), bf16),
            pltpu.VMEM((8, rows, width - early), bf16),
            pltpu.VMEM((4, 2, width // LANES, rows, LANES), bf16),
            pltpu.VMEM((4, 2, width // LANES, rows, LANES), bf16),
            pltpu.SemaphoreType.DMA((7,)),
            pltpu.SemaphoreType.DMA((copies,)),
            pltpu.SemaphoreType.DMA((copies,)),
            pltpu.SemaphoreType.DMA((hops,)),
            pltpu.SemaphoreType.DMA((hops,)),
        ],
        compiler_params=pltpu.CompilerParams(
            collective_id=0, has_side_effects=True, vmem_limit_bytes=60 * 1024 * 1024
        ),
        name="block",
    )(
        queries, key_rows, value_rows, ref_keys, ref_values, key_lists, list_counts, owner_index, out_weight,
    )
    return (residual.astype(f32) + gate_scale[None, :] * projected).astype(bf16)


def solution(mesh):
    placed = (
        P("frame", "head"),
        P("frame", "head"),
        P("frame", "head"),
        P("frame", None, "head"),
        P("frame", None, "head"),
        P("frame", None),
        P("frame"),
        P(),
        P("head", None),
        P("frame", "head"),
        P("head"),
    )
    return jax.shard_map(
        per_device, mesh=mesh, in_specs=placed, out_specs=P("frame", "head"), check_vma=False
    )
```

time: 76.4 us -> 81.7 us (1.069)
  the two profiles are of different devices: /device:TPU:8 before, /device:TPU:1 now
where the time goes in v3:
time: 81.7 us; the launch traced here: 81.6 us
  Pallas kernels  78.5 us (96%)
  other arithmetic  1.69 us (2%)
  between operations  1.34 us (2%)
    pallas_call x1, Pallas kernels, per_device(): pl.pallas_call(kernel, out_shape=jax.ShapeDtypeStruct((rows, width), f32)...  78.5 us
    convert_element_type x1, other arithmetic, per_device(): return (residual.astype(f32) + gate_scale[None, :] * projected).astype(bf16)  1.69 us

profile of v3, /device:TPU:1, one launch (start us, length us, event | category | flops | bytes accessed | tf_op | source)
XLA Modules:
  0.0 81.6 jit_solution(7613409229054299229)
XLA Ops:
  1.3 0.0 copy-start
  1.3 0.0 copy-start.1
  1.3 78.5 %block.1 = f32[224,384]{1,0:T(8,128)} custom-call(bf16[224,384]{1,0:T(8,128)(2,1)} %q_hbm.1, bf16[224,384]{1,0:T(8,128)(2,1)} %k_hbm.1, bf16[224,384]{1,0:T(8,128)(2,1)} %v_hbm.1, bf16[1,1024,384]{2,1,0:T(8,128)(2,1)} %rk_hbm.1, bf16[1,1024,384]{2,1,0:T(8,128)(2,1)} %rv_hbm.1, s32[1,8]{1,0:T(1,128)} %lists.1, s32[1]{0:T(128)S(6)} %copy.12.counts, ...), custom_call_target="tpu_custom_call" | custom-call | tf_op jit(solution)/shard_map/block/pallas_call | solution.py:440
  79.9 0.0 copy-done
  79.9 0.0 copy-done.1
  79.9 1.7 %add_convert_fusion = bf16[224,384]{1,0:T(8,128)(2,1)} fusion(f32[224,384]{1,0:T(8,128)} %block.1, bf16[224,384]{1,0:T(8,128)(2,1)S(1)} %copy-done, f32[384]{0:T(512)S(1)} %copy-done.1), kind=kLoop, calls=%fused_computation | loop fusion | flops 344064 | bytes 689664 | tf_op jit(solution)/shard_map/convert_element_type | solution.py:478
Async XLA Ops:
  1.3 78.6 %copy-start = (bf16[224,384]{1,0:T(8,128)(2,1)S(1)}, bf16[224,384]{1,0:T(8,128)(2,1)}, u32[]{:S(2)}) copy-start(bf16[224,384]{1,0:T(8,128)(2,1)} %param.20) | copy-start | bytes 516100
  1.3 78.6 %copy-start.1 = (f32[384]{0:T(512)S(1)}, f32[384]{0:T(512)}, u32[]{:S(2)}) copy-start(f32[384]{0:T(512)} %param.21) | copy-start | bytes 4612

commit v4 on v3

--- a/solution.py
+++ b/solution.py
@@ -23,17 +23,14 @@
     q_hbm, k_hbm, v_hbm, rk_hbm, rv_hbm, lists, counts, owner, w_hbm,
     out_ref,
     q_buf, k_near, v_near, ref_own, ref_sib, ref_sel, x_parts, x_sum, y_parts, style,
-    w_sum, w_all, top, total, acc, att, att_all, z_out, z_in, local_sem, send_sem, recv_sem, z_send, z_recv,
+    w_sum, top, total, acc, att, z_out, z_in, local_sem, send_sem, recv_sem, z_send, z_recv,
 ):
     rows, width = q_buf.shape
     slots = lists.shape[1]
     ref_rows = style.shape[1]
     half = rows // 2
     block, bit = ref_rows // 8, ref_rows // 32
-    early = w_sum.shape[0]
-    cols = (pl.ds(0, early), pl.ds(early, width - early))
-    heads = (tuple(range(early // HD)), tuple(range(early // HD, width // HD)))
-    late = width - early
+    cols, heads = (pl.ds(0, width),), (tuple(range(width // HD)),)
 
     frame = lax.axis_index("frame")
     z = lax.axis_index("head")
@@ -106,12 +103,10 @@
             for s in (0, 1):
                 keep(s, which).start()
 
-    get_w = fetch(w_hbm.at[pl.ds(0, early)], w_sum, 5)
+    get_w = fetch(w_hbm, w_sum, 5)
 
     def column_block(o):
         return pl.ds(pl.multiple_of(ahead(o) * width, LANES), width)
-
-    get_own_w = fetch(w_hbm.at[pl.ds(early, late), column_block(0)], w_all.at[z], 6)
 
     barrier = pltpu.get_barrier_semaphore()
     partners = (
@@ -119,13 +114,13 @@
         + [at_x(j) for j in (1, 2, 3)]
         + [at_y(j) for j in (1, 2, 3)]
         + [at_chip(o) for o in (1, -1)]
-        + [at_z(o) for o in range(1, 8)]
+        + [at_z(1), at_z(-1)]
     )
     for device in partners:
         pl.semaphore_signal(barrier, inc=1, device_id=device, device_id_type=MESH)
     pl.semaphore_wait(barrier, len(partners))
 
-    gifts = [(s, w) for w in (0, 1) for s in (0, 1)]
+    gifts = [(s, w) for w in (0,) for s in (0, 1)]
     for which in (0, 1):
 
         @pl.when(core == which)
@@ -165,9 +160,6 @@
         ]
 
     to_next(0, k_hbm, k_near)
-    w_moves = {
-        o: send(w_hbm.at[pl.ds(early, late), column_block(o)], w_all.at[z], at_z(o)) for o in (4, 3, 5, 2, 6, 1, 7)
-    }
 
     top[...] = jnp.full(top.shape, -FAR, jnp.float32)
     total[...] = jnp.zeros(total.shape, jnp.float32)
@@ -320,51 +312,24 @@
                     )
                 hop(way, step, part).start()
 
-    spread = {}
-
-    def gather_near():
-        mine_here = att.at[:, cols[1]]
-        for o in (2, -2, 1, -1):
-            spread[o] = send(mine_here, att_all.at[z], at_z(o))
-
-    def gather_far():
-        for way in (0, 1):
-            o = signs[way]
-            spread[2 * o].wait_recv()
-            origin = ahead(-2 * o)
-            some = pl.ds(way * half, half)
-            spread[4 * o] = send(att_all.at[origin, some], att_all.at[origin, some], at_z(2 * o))
-            spread[3 * o] = send(att_all.at[origin], att_all.at[origin], at_z(o))
-
-    def late_share(o):
-        return dot(att_all[ahead(o)], w_all[ahead(o)], ((1,), (0,)))
-
     both(choose, 0)
-    to_next(0, v_hbm, v_near)
     get_q.wait()
     get_k.wait()
     get_v.wait()
     for copy in to_sib:
         copy.wait_recv()
     absorb(0, [(k_near.at[own], v_near.at[own], None), near_block(5 - core)])
+    to_next(0, v_hbm, v_near)
+    both(narrow, 0)
     relay(0)
-    to_next(1, k_hbm, k_near)
-    to_next(1, v_hbm, v_near)
-    both(choose, 1)
-    absorb(1, [(k_near.at[own], v_near.at[own], None), near_block(5 - core)])
-    both(narrow, 0)
     absorb_near(0, slot_of(-1), slot_of(1))
     both(settle, 0)
-    both(narrow, 1)
     for copy in passed[0]:
         copy.wait_recv()
     absorb_near(0, 3 - core, 7 - core)
     both(widen, 0)
-    both(settle, 1)
     relay_far(0)
-    relay(1)
     absorb_near(0, slot_of(-2), slot_of(2))
-    both(widen, 1)
     for copy in gone[0]:
         copy.wait_recv()
     absorb_near(0, 1 + 7 * core)
@@ -375,44 +340,14 @@
         absorb_style(0, j)
     finish(0)
     get_w.wait()
-    climb(0)
-    absorb_near(1, slot_of(-1), slot_of(1))
-    for copy in passed[1]:
-        copy.wait_recv()
-    absorb_near(1, 3 - core, 7 - core)
-    climb(1)
-    relay_far(1)
-    absorb_near(1, slot_of(-2), slot_of(2))
-    absorb_style(1, 0)
-    for j in order:
-        for s in (0, 1):
-            show(s, 1, j)
-    climb(2)
-    for copy in gone[1]:
-        copy.wait_recv()
-    absorb_near(1, 1 + 7 * core)
-    for j in order:
-        absorb_style(1, j)
-    finish(1)
-    gather_near()
-    climb(3)
-    att_all[z] = att[:, cols[1]]
-    get_own_w.wait()
-    for copy in w_moves.values():
-        copy.wait_recv()
-    out_ref[...] = share(0, whole) + late_share(0)
-    gather_far()
-    for o in (1, -1):
-        spread[o].wait_recv()
-    out_ref[...] += late_share(1) + late_share(-1) + late_share(2) + late_share(-2)
+    for step in range(4):
+        climb(step)
+    out_ref[...] = share(0, whole)
     for part in range(parts):
         lanes = pl.ds(part * LANES, LANES)
         for way in (0, 1):
             hop(way, 3, part).wait_recv()
         out_ref[:, lanes] += z_in[3, 0, part].astype(jnp.float32) + z_in[3, 1, part].astype(jnp.float32)
-    for o in (3, -3, 4, -4):
-        spread[o].wait_recv()
-    out_ref[...] += late_share(3) + late_share(-3) + late_share(4)
 
     for copy in made:
         copy.wait_send()
@@ -428,14 +363,13 @@
 ):
     rows, width = queries.shape
     heads = width // HD
-    early = (heads - 1) * HD
     ref_rows = ref_keys.shape[1]
     block, bit = ref_rows // 8, ref_rows // 32
     bf16, f32 = jnp.bfloat16, jnp.float32
     hbm = pl.BlockSpec(memory_space=pl.ANY)
     vmem = pl.BlockSpec(memory_space=pltpu.VMEM)
     smem = pl.BlockSpec(memory_space=pltpu.SMEM)
-    copies = 128
+    copies = 72
     hops = 4 * 2 * (width // LANES)
     projected = pl.pallas_call(
         kernel,
@@ -453,13 +387,11 @@
             pltpu.VMEM((2, block, width), bf16),
             pltpu.VMEM((2, 3, bit, width), bf16),
             pltpu.VMEM((2, ref_rows, width), bf16),
-            pltpu.VMEM((early, out_weight.shape[1]), bf16),
-            pltpu.VMEM((8, width - early, width), bf16),
+            pltpu.VMEM(out_weight.shape, bf16),
             pltpu.VMEM((heads, 1, rows), f32),
             pltpu.VMEM((heads, 1, rows), f32),
             pltpu.VMEM((heads, HD, rows), f32),
             pltpu.VMEM((rows, width), bf16),
-            pltpu.VMEM((8, rows, width - early), bf16),
             pltpu.VMEM((4, 2, width // LANES, rows, LANES), bf16),
             pltpu.VMEM((4, 2, width // LANES, rows, LANES), bf16),
             pltpu.SemaphoreType.DMA((7,)),

time: 81.7 us -> 74.4 us (0.911)
  the two profiles are of different devices: /device:TPU:1 before, /device:TPU:8 now
where the time goes in v4:
time: 74.4 us; the launch traced here: 73 us
  Pallas kernels  69.9 us (94%)
  other arithmetic  1.69 us (2%)
  between operations  1.34 us (2%)
    pallas_call x1, Pallas kernels, per_device(): pl.pallas_call(kernel, out_shape=jax.ShapeDtypeStruct((rows, width), f32)...  69.9 us
    convert_element_type x1, other arithmetic, per_device(): return (residual.astype(f32) + gate_scale[None, :] * projected).astype(bf16)  1.69 us

profile of v4, /device:TPU:8, one launch (start us, length us, event | category | flops | bytes accessed | tf_op | source)
XLA Modules:
  0.0 73.0 jit_solution(10779097100640742484)
XLA Ops:
  1.3 0.0 copy-start
  1.3 0.0 copy-start.1
  1.3 69.9 %block.1 = f32[224,384]{1,0:T(8,128)} custom-call(bf16[224,384]{1,0:T(8,128)(2,1)} %q_hbm.1, bf16[224,384]{1,0:T(8,128)(2,1)} %k_hbm.1, bf16[224,384]{1,0:T(8,128)(2,1)} %v_hbm.1, bf16[1,1024,384]{2,1,0:T(8,128)(2,1)} %rk_hbm.1, bf16[1,1024,384]{2,1,0:T(8,128)(2,1)} %rv_hbm.1, s32[1,8]{1,0:T(1,128)} %lists.1, s32[1]{0:T(128)S(6)} %copy.12.counts, ...), custom_call_target="tpu_custom_call" | custom-call | tf_op jit(solution)/shard_map/block/pallas_call | solution.py:374
  71.3 0.0 copy-done
  71.3 0.0 copy-done.1
  71.3 1.7 %add_convert_fusion = bf16[224,384]{1,0:T(8,128)(2,1)} fusion(f32[224,384]{1,0:T(8,128)} %block.1, bf16[224,384]{1,0:T(8,128)(2,1)S(1)} %copy-done, f32[384]{0:T(512)S(1)} %copy-done.1), kind=kLoop, calls=%fused_computation | loop fusion | flops 344064 | bytes 689664 | tf_op jit(solution)/shard_map/convert_element_type | solution.py:410
Async XLA Ops:
  1.3 70.0 %copy-start = (bf16[224,384]{1,0:T(8,128)(2,1)S(1)}, bf16[224,384]{1,0:T(8,128)(2,1)}, u32[]{:S(2)}) copy-start(bf16[224,384]{1,0:T(8,128)(2,1)} %param.20) | copy-start | bytes 516100
  1.3 70.0 %copy-start.1 = (f32[384]{0:T(512)S(1)}, f32[384]{0:T(512)}, u32[]{:S(2)}) copy-start(f32[384]{0:T(512)} %param.21) | copy-start | bytes 4612

commit v5 on v4

--- a/solution.py
+++ b/solution.py
@@ -290,13 +290,13 @@
         )
 
     def climb(step):
-        for way in (0, 1):
-            some = pl.ds(way * half, half) if step == 0 else whole
-            here_share = share(signs[way] * (4 - step), some)
-            for part in range(parts):
-                value = here_share[:, part * LANES : (part + 1) * LANES]
+        some = [pl.ds(way * half, half) if step == 0 else whole for way in (0, 1)]
+        shares = [share(signs[way] * (4 - step), some[way]) for way in (0, 1)]
+        for part in range(parts):
+            for way in (0, 1):
+                value = shares[way][:, part * LANES : (part + 1) * LANES]
                 if step == 0:
-                    z_out[step, way, part, some] = value.astype(jnp.bfloat16)
+                    z_out[step, way, part, some[way]] = value.astype(jnp.bfloat16)
                 elif step == 1:
                     hop(way, 0, part).wait_recv()
                     for which in (0, 1):
@@ -334,10 +334,15 @@
         copy.wait_recv()
     absorb_near(0, 1 + 7 * core)
     absorb_style(0, 0)
-    for j in order:
-        for s in (0, 1):
-            show(s, 0, j)
-        absorb_style(0, j)
+    for s in (0, 1):
+        show(s, 0, 1)
+    for s in (0, 1):
+        show(s, 0, 3)
+    absorb_style(0, 1)
+    for s in (0, 1):
+        show(s, 0, 2)
+    absorb_style(0, 3)
+    absorb_style(0, 2)
     finish(0)
     get_w.wait()
     for step in range(4):

time: 74.4 us -> 69.6 us (0.935); the launches traced: 73 us -> 69.4 us
  Pallas kernels: 69.9 us -> 66.4 us
    pallas_call x1, Pallas kernels: 69.9 us -> 66.4 us  [per_device(): pl.pallas_call(kernel, out_shape=jax.ShapeDtypeStruct((rows, width), f32)...]
where the time goes in v5:
time: 69.6 us; the launch traced here: 69.4 us
  Pallas kernels  66.4 us (95%)
  other arithmetic  1.69 us (2%)
  between operations  1.34 us (2%)
    pallas_call x1, Pallas kernels, per_device(): pl.pallas_call(kernel, out_shape=jax.ShapeDtypeStruct((rows, width), f32)...  66.4 us
    convert_element_type x1, other arithmetic, per_device(): return (residual.astype(f32) + gate_scale[None, :] * projected).astype(bf16)  1.69 us

profile of v5, /device:TPU:8, one launch (start us, length us, event | category | flops | bytes accessed | tf_op | source)
XLA Modules:
  0.0 69.4 jit_solution(7969212723244356426)
XLA Ops:
  1.3 0.0 copy-start
  1.3 0.0 copy-start.1
  1.3 66.4 %block.1 = f32[224,384]{1,0:T(8,128)} custom-call(bf16[224,384]{1,0:T(8,128)(2,1)} %q_hbm.1, bf16[224,384]{1,0:T(8,128)(2,1)} %k_hbm.1, bf16[224,384]{1,0:T(8,128)(2,1)} %v_hbm.1, bf16[1,1024,384]{2,1,0:T(8,128)(2,1)} %rk_hbm.1, bf16[1,1024,384]{2,1,0:T(8,128)(2,1)} %rv_hbm.1, s32[1,8]{1,0:T(1,128)} %lists.1, s32[1]{0:T(128)S(6)} %copy.12.counts, ...), custom_call_target="tpu_custom_call" | custom-call | tf_op jit(solution)/shard_map/block/pallas_call | solution.py:379
  67.7 0.0 copy-done
  67.7 0.0 copy-done.1
  67.7 1.7 %add_convert_fusion = bf16[224,384]{1,0:T(8,128)(2,1)} fusion(f32[224,384]{1,0:T(8,128)} %block.1, bf16[224,384]{1,0:T(8,128)(2,1)S(1)} %copy-done, f32[384]{0:T(512)S(1)} %copy-done.1), kind=kLoop, calls=%fused_computation | loop fusion | flops 344064 | bytes 689664 | tf_op jit(solution)/shard_map/convert_element_type | solution.py:415
Async XLA Ops:
  1.3 66.4 %copy-start = (bf16[224,384]{1,0:T(8,128)(2,1)S(1)}, bf16[224,384]{1,0:T(8,128)(2,1)}, u32[]{:S(2)}) copy-start(bf16[224,384]{1,0:T(8,128)(2,1)} %param.20) | copy-start | bytes 516100
  1.3 66.4 %copy-start.1 = (f32[384]{0:T(512)S(1)}, f32[384]{0:T(512)}, u32[]{:S(2)}) copy-start(f32[384]{0:T(512)} %param.21) | copy-start | bytes 4612

commit v6 on v5

--- a/solution.py
+++ b/solution.py
@@ -29,7 +29,9 @@
     slots = lists.shape[1]
     ref_rows = style.shape[1]
     half = rows // 2
-    block, bit = ref_rows // 8, ref_rows // 32
+    chains = 4
+    base, size = tuple(ref_rows // chains * s for s in range(chains)), (ref_rows // chains,) * chains
+    block, bit = tuple(n // 4 for n in size), tuple(n // 16 for n in size)
     cols, heads = (pl.ds(0, width),), (tuple(range(width // HD)),)
 
     frame = lax.axis_index("frame")
@@ -76,6 +78,7 @@
         return copy
 
     own = 4 + core
+    sooner, later = (0, 2), (1, 3)
     get_q = fetch(q_hbm, q_buf, 0)
     get_k = fetch(k_hbm, k_near.at[own], 1)
     get_v = fetch(v_hbm, v_near.at[own], 2)
@@ -83,7 +86,7 @@
     style_in = ((rk_hbm, rv_hbm), (rv_hbm, rk_hbm))
 
     def half_rows(s):
-        return pl.ds(s * 4 * block, 4 * block)
+        return pl.ds(base[s], size[s])
 
     def keep(s, which):
         return pltpu.make_async_copy(
@@ -100,10 +103,10 @@
 
         @pl.when(core == which)
         def _():
-            for s in (0, 1):
+            for s in sooner + later:
                 keep(s, which).start()
 
-    get_w = fetch(w_hbm, w_sum, 5)
+    get_w = fetch(w_hbm, w_sum, 7)
 
     def column_block(o):
         return pl.ds(pl.multiple_of(ahead(o) * width, LANES), width)
@@ -120,7 +123,7 @@
         pl.semaphore_signal(barrier, inc=1, device_id=device, device_id_type=MESH)
     pl.semaphore_wait(barrier, len(partners))
 
-    gifts = [(s, w) for w in (0,) for s in (0, 1)]
+    gifts = [(s, w) for w in (0,) for s in sooner + later]
     for which in (0, 1):
 
         @pl.when(core == which)
@@ -198,23 +201,26 @@
     def absorb_near(w, *which):
         absorb(w, [near_block(slot) for slot in which])
 
-    first_axis, first_at, second_axis, second_at = (x, y), (at_x, at_y), (y, x), (at_y, at_x)
+    first_axis, first_at = (x, x, y, y), (at_x, at_x, at_y, at_y)
+    second_axis, second_at = (y, y, x, x), (at_y, at_y, at_x, at_x)
     order = (1, 3, 2)
     mine = jnp.where(owner[0] == frame, 1.0, 0.0).astype(jnp.bfloat16)
     theirs = jnp.where(owner[0] == frame + 1 - 2 * core, 1.0, 0.0).astype(jnp.bfloat16)
     carried = style.at[core]
 
     def block_rows(s, j):
-        return pl.ds(pl.multiple_of(s * 4 * block + lax.rem(first_axis[s] + j, 4) * block, block), block)
+        return pl.ds(pl.multiple_of(base[s] + lax.rem(first_axis[s] + j, 4) * block[s], bit[s]), block[s])
 
     def bit_rows(s, j):
-        return pl.ds(pl.multiple_of(lax.rem(second_axis[s] + j, 4) * bit, bit), bit)
+        return pl.ds(pl.multiple_of(lax.rem(second_axis[s] + j, 4) * bit[s], bit[s]), bit[s])
 
     def own_bit(s):
         return pl.ds(
-            pl.multiple_of(s * 4 * block + first_axis[s] * block + second_axis[s] * bit, bit), bit
-        )
-
+            pl.multiple_of(base[s] + first_axis[s] * block[s] + second_axis[s] * bit[s], bit[s]), bit[s]
+        )
+
+    whole_block = tuple(pl.ds(0, n) for n in block)
+    whole_bit = tuple(pl.ds(0, n) for n in bit)
     chosen, narrowed, settled, widened, shown = {}, {}, {}, {}, {}
 
     def choose(s, w):
@@ -224,26 +230,28 @@
         given[s, w].wait_recv()
         ref_sel[r, c] = ref_own[r, c] * mine + ref_sib[r, c] * theirs
         chosen[s, w] = [
-            send(ref_sel.at[block_rows(s, j), c], x_parts.at[s, j - 1, :, c], first_at[s](j)) for j in order
+            send(ref_sel.at[block_rows(s, j), c], x_parts.at[s, j - 1, whole_block[s], c], first_at[s](j)) for j in order
         ]
 
     def narrow(s, w):
         c = cols[w]
         for copy in chosen[s, w]:
             copy.wait_recv()
-        x_sum[s, :, c] = (
-            ref_sel[block_rows(s, 0), c] + x_parts[s, 0, :, c] + x_parts[s, 1, :, c] + x_parts[s, 2, :, c]
+        b = whole_block[s]
+        x_sum[s, b, c] = (
+            ref_sel[block_rows(s, 0), c] + x_parts[s, 0, b, c] + x_parts[s, 1, b, c] + x_parts[s, 2, b, c]
         )
         narrowed[s, w] = [
-            send(x_sum.at[s, bit_rows(s, j), c], y_parts.at[s, j - 1, :, c], second_at[s](j)) for j in order
+            send(x_sum.at[s, bit_rows(s, j), c], y_parts.at[s, j - 1, whole_bit[s], c], second_at[s](j)) for j in order
         ]
 
     def settle(s, w):
         c = cols[w]
         for copy in narrowed[s, w]:
             copy.wait_recv()
+        b = whole_bit[s]
         carried[own_bit(s), c] = (
-            x_sum[s, bit_rows(s, 0), c] + y_parts[s, 0, :, c] + y_parts[s, 1, :, c] + y_parts[s, 2, :, c]
+            x_sum[s, bit_rows(s, 0), c] + y_parts[s, 0, b, c] + y_parts[s, 1, b, c] + y_parts[s, 2, b, c]
         )
         here = carried.at[own_bit(s), c]
         settled[s, w] = [send(here, here, second_at[s](j)) for j in order]
@@ -261,13 +269,15 @@
         shown[s, w, j] = send(there, there, sibling)
 
     def absorb_style(w, j):
-        for s in (0, 1):
+        for s in range(chains):
             shown[s, w, j].wait_recv()
-        absorb(w, [(style.at[0, block_rows(s, 4 - j)], style.at[1, block_rows(s, 4 - j)], None) for s in (0, 1)])
-
-    def both(stage, w):
-        for s in (0, 1):
-            stage(s, w)
+        absorb(
+            w, [(style.at[0, block_rows(s, 4 - j)], style.at[1, block_rows(s, 4 - j)], None) for s in range(chains)]
+        )
+
+    def both(stage, which):
+        for s in which:
+            stage(s, 0)
 
     def finish(w):
         for h in heads[w]:
@@ -312,7 +322,8 @@
                     )
                 hop(way, step, part).start()
 
-    both(choose, 0)
+    both(choose, sooner)
+    both(choose, later)
     get_q.wait()
     get_k.wait()
     get_v.wait()
@@ -320,26 +331,28 @@
         copy.wait_recv()
     absorb(0, [(k_near.at[own], v_near.at[own], None), near_block(5 - core)])
     to_next(0, v_hbm, v_near)
-    both(narrow, 0)
+    both(narrow, sooner)
+    both(narrow, later)
     relay(0)
     absorb_near(0, slot_of(-1), slot_of(1))
-    both(settle, 0)
+    both(settle, sooner)
+    both(settle, later)
     for copy in passed[0]:
         copy.wait_recv()
     absorb_near(0, 3 - core, 7 - core)
-    both(widen, 0)
+    both(widen, sooner)
+    both(widen, later)
     relay_far(0)
     absorb_near(0, slot_of(-2), slot_of(2))
     for copy in gone[0]:
         copy.wait_recv()
     absorb_near(0, 1 + 7 * core)
     absorb_style(0, 0)
-    for s in (0, 1):
-        show(s, 0, 1)
-    for s in (0, 1):
-        show(s, 0, 3)
+    for j in (1, 3):
+        for s in sooner + later:
+            show(s, 0, j)
     absorb_style(0, 1)
-    for s in (0, 1):
+    for s in sooner + later:
         show(s, 0, 2)
     absorb_style(0, 3)
     absorb_style(0, 2)
@@ -369,12 +382,12 @@
     rows, width = queries.shape
     heads = width // HD
     ref_rows = ref_keys.shape[1]
-    block, bit = ref_rows // 8, ref_rows // 32
+    block, bit = ref_rows // 16, ref_rows // 64
     bf16, f32 = jnp.bfloat16, jnp.float32
     hbm = pl.BlockSpec(memory_space=pl.ANY)
     vmem = pl.BlockSpec(memory_space=pltpu.VMEM)
     smem = pl.BlockSpec(memory_space=pltpu.SMEM)
-    copies = 72
+    copies = 96
     hops = 4 * 2 * (width // LANES)
     projected = pl.pallas_call(
         kernel,
@@ -388,9 +401,9 @@
             pltpu.VMEM((ref_rows, width), bf16),
             pltpu.VMEM((ref_rows, width), bf16),
             pltpu.VMEM((ref_rows, width), bf16),
-            pltpu.VMEM((2, 3, block, width), bf16),
-            pltpu.VMEM((2, block, width), bf16),
-            pltpu.VMEM((2, 3, bit, width), bf16),
+            pltpu.VMEM((4, 3, block, width), bf16),
+            pltpu.VMEM((4, block, width), bf16),
+            pltpu.VMEM((4, 3, bit, width), bf16),
             pltpu.VMEM((2, ref_rows, width), bf16),
             pltpu.VMEM(out_weight.shape, bf16),
             pltpu.VMEM((heads, 1, rows), f32),
@@ -399,7 +412,7 @@
             pltpu.VMEM((rows, width), bf16),
             pltpu.VMEM((4, 2, width // LANES, rows, LANES), bf16),
             pltpu.VMEM((4, 2, width // LANES, rows, LANES), bf16),
-            pltpu.SemaphoreType.DMA((7,)),
+            pltpu.SemaphoreType.DMA((8,)),
             pltpu.SemaphoreType.DMA((copies,)),
             pltpu.SemaphoreType.DMA((copies,)),
             pltpu.SemaphoreType.DMA((hops,)),

time: 69.6 us -> 68.8 us (0.989); the launches traced: 69.4 us -> 67.5 us
  Pallas kernels: 66.4 us -> 64.5 us
    pallas_call x1, Pallas kernels: 66.4 us -> 64.5 us  [per_device(): pl.pallas_call(kernel, out_shape=jax.ShapeDtypeStruct((rows, width), f32)...]
where the time goes in v6:
time: 68.8 us; the launch traced here: 67.5 us
  Pallas kernels  64.5 us (94%)
  other arithmetic  1.69 us (2%)
  between operations  1.34 us (2%)
    pallas_call x1, Pallas kernels, per_device(): pl.pallas_call(kernel, out_shape=jax.ShapeDtypeStruct((rows, width), f32)...  64.5 us
    convert_element_type x1, other arithmetic, per_device(): return (residual.astype(f32) + gate_scale[None, :] * projected).astype(bf16)  1.69 us

profile of v6, /device:TPU:8, one launch (start us, length us, event | category | flops | bytes accessed | tf_op | source)
XLA Modules:
  0.0 67.5 jit_solution(12806503274790698049)
XLA Ops:
  1.3 0.0 copy-start
  1.3 0.0 copy-start.1
  1.3 64.5 %block.1 = f32[224,384]{1,0:T(8,128)} custom-call(bf16[224,384]{1,0:T(8,128)(2,1)} %q_hbm.1, bf16[224,384]{1,0:T(8,128)(2,1)} %k_hbm.1, bf16[224,384]{1,0:T(8,128)(2,1)} %v_hbm.1, bf16[1,1024,384]{2,1,0:T(8,128)(2,1)} %rk_hbm.1, bf16[1,1024,384]{2,1,0:T(8,128)(2,1)} %rv_hbm.1, s32[1,8]{1,0:T(1,128)} %lists.1, s32[1]{0:T(128)S(6)} %copy.12.counts, ...), custom_call_target="tpu_custom_call" | custom-call | tf_op jit(solution)/shard_map/block/pallas_call | solution.py:392
  65.8 0.0 copy-done
  65.8 0.0 copy-done.1
  65.8 1.7 %add_convert_fusion = bf16[224,384]{1,0:T(8,128)(2,1)} fusion(f32[224,384]{1,0:T(8,128)} %block.1, bf16[224,384]{1,0:T(8,128)(2,1)S(1)} %copy-done, f32[384]{0:T(512)S(1)} %copy-done.1), kind=kLoop, calls=%fused_computation | loop fusion | flops 344064 | bytes 689664 | tf_op jit(solution)/shard_map/convert_element_type | solution.py:428
Async XLA Ops:
  1.3 64.5 %copy-start = (bf16[224,384]{1,0:T(8,128)(2,1)S(1)}, bf16[224,384]{1,0:T(8,128)(2,1)}, u32[]{:S(2)}) copy-start(bf16[224,384]{1,0:T(8,128)(2,1)} %param.20) | copy-start | bytes 516100
  1.3 64.5 %copy-start.1 = (f32[384]{0:T(512)S(1)}, f32[384]{0:T(512)}, u32[]{:S(2)}) copy-start(f32[384]{0:T(512)} %param.21) | copy-start | bytes 4612

commit v7 on v6

--- a/solution.py
+++ b/solution.py
@@ -214,10 +214,15 @@
     def bit_rows(s, j):
         return pl.ds(pl.multiple_of(lax.rem(second_axis[s] + j, 4) * bit[s], bit[s]), bit[s])
 
+    def place_of(s, j):
+        first = s - s % 2
+        return base[first] + lax.rem(first_axis[s] + j, 4) * (2 * block[s]) + s % 2 * block[s]
+
+    def place(s, j):
+        return pl.ds(pl.multiple_of(place_of(s, j), block[s]), block[s])
+
     def own_bit(s):
-        return pl.ds(
-            pl.multiple_of(base[s] + first_axis[s] * block[s] + second_axis[s] * bit[s], bit[s]), bit[s]
-        )
+        return pl.ds(pl.multiple_of(place_of(s, 0) + second_axis[s] * bit[s], bit[s]), bit[s])
 
     whole_block = tuple(pl.ds(0, n) for n in block)
     whole_bit = tuple(pl.ds(0, n) for n in bit)
@@ -259,21 +264,23 @@
     def widen(s, w):
         for copy in settled[s, w]:
             copy.wait_recv()
-        here = carried.at[block_rows(s, 0), cols[w]]
+        here = carried.at[place(s, 0), cols[w]]
         widened[s, w] = {j: send(here, here, first_at[s](j)) for j in order}
         shown[s, w, 0] = send(here, here, sibling)
 
     def show(s, w, j):
         widened[s, w][j].wait_recv()
-        there = carried.at[block_rows(s, 4 - j), cols[w]]
+        there = carried.at[place(s, 4 - j), cols[w]]
         shown[s, w, j] = send(there, there, sibling)
 
     def absorb_style(w, j):
         for s in range(chains):
             shown[s, w, j].wait_recv()
-        absorb(
-            w, [(style.at[0, block_rows(s, 4 - j)], style.at[1, block_rows(s, 4 - j)], None) for s in range(chains)]
-        )
+        blocks = []
+        for s in range(0, chains, 2):
+            rows_of = pl.ds(pl.multiple_of(place_of(s, 4 - j), 2 * block[s]), 2 * block[s])
+            blocks.append((style.at[0, rows_of], style.at[1, rows_of], None))
+        absorb(w, blocks)
 
     def both(stage, which):
         for s in which:

time: 68.8 us -> 68.3 us (level)
  no operation moved by 1% of the time
where the time goes in v7:
time: 68.3 us; the launch traced here: 67.1 us
  Pallas kernels  64 us (94%)
  other arithmetic  1.69 us (2%)
  between operations  1.34 us (2%)
    pallas_call x1, Pallas kernels, per_device(): pl.pallas_call(kernel, out_shape=jax.ShapeDtypeStruct((rows, width), f32)...  64 us
    convert_element_type x1, other arithmetic, per_device(): return (residual.astype(f32) + gate_scale[None, :] * projected).astype(bf16)  1.69 us

profile of v7, /device:TPU:8, one launch (start us, length us, event | category | flops | bytes accessed | tf_op | source)
XLA Modules:
  0.0 67.1 jit_solution(7889954752356958628)
XLA Ops:
  1.3 0.0 copy-start
  1.3 0.0 copy-start.1
  1.3 64.0 %block.1 = f32[224,384]{1,0:T(8,128)} custom-call(bf16[224,384]{1,0:T(8,128)(2,1)} %q_hbm.1, bf16[224,384]{1,0:T(8,128)(2,1)} %k_hbm.1, bf16[224,384]{1,0:T(8,128)(2,1)} %v_hbm.1, bf16[1,1024,384]{2,1,0:T(8,128)(2,1)} %rk_hbm.1, bf16[1,1024,384]{2,1,0:T(8,128)(2,1)} %rv_hbm.1, s32[1,8]{1,0:T(1,128)} %lists.1, s32[1]{0:T(128)S(6)} %copy.12.counts, ...), custom_call_target="tpu_custom_call" | custom-call | tf_op jit(solution)/shard_map/block/pallas_call | solution.py:399
  65.3 0.0 copy-done
  65.4 0.0 copy-done.1
  65.4 1.7 %add_convert_fusion = bf16[224,384]{1,0:T(8,128)(2,1)} fusion(f32[224,384]{1,0:T(8,128)} %block.1, bf16[224,384]{1,0:T(8,128)(2,1)S(1)} %copy-done, f32[384]{0:T(512)S(1)} %copy-done.1), kind=kLoop, calls=%fused_computation | loop fusion | flops 344064 | bytes 689664 | tf_op jit(solution)/shard_map/convert_element_type | solution.py:435
Async XLA Ops:
  1.3 64.1 %copy-start = (bf16[224,384]{1,0:T(8,128)(2,1)S(1)}, bf16[224,384]{1,0:T(8,128)(2,1)}, u32[]{:S(2)}) copy-start(bf16[224,384]{1,0:T(8,128)(2,1)} %param.20) | copy-start | bytes 516100
  1.3 64.1 %copy-start.1 = (f32[384]{0:T(512)S(1)}, f32[384]{0:T(512)}, u32[]{:S(2)}) copy-start(f32[384]{0:T(512)} %param.21) | copy-start | bytes 4612

commit v8 on v7

--- a/solution.py
+++ b/solution.py
@@ -329,15 +329,22 @@
                     )
                 hop(way, step, part).start()
 
+    def drain(steps):
+        for step in steps:
+            for way in (0, 1):
+                for part in range(parts):
+                    hop(way, step, part).wait_send()
+
     both(choose, sooner)
-    both(choose, later)
     get_q.wait()
     get_k.wait()
     get_v.wait()
+    absorb(0, [(k_near.at[own], v_near.at[own], None)])
+    both(choose, later)
+    to_next(0, v_hbm, v_near)
     for copy in to_sib:
         copy.wait_recv()
-    absorb(0, [(k_near.at[own], v_near.at[own], None), near_block(5 - core)])
-    to_next(0, v_hbm, v_near)
+    absorb_near(0, 5 - core)
     both(narrow, sooner)
     both(narrow, later)
     relay(0)
@@ -367,19 +374,20 @@
     get_w.wait()
     for step in range(4):
         climb(step)
-    out_ref[...] = share(0, whole)
+        for copy in made[step::4]:
+            copy.wait_send()
+    mine_here = share(0, whole)
+    drain(range(3))
     for part in range(parts):
         lanes = pl.ds(part * LANES, LANES)
         for way in (0, 1):
             hop(way, 3, part).wait_recv()
-        out_ref[:, lanes] += z_in[3, 0, part].astype(jnp.float32) + z_in[3, 1, part].astype(jnp.float32)
-
-    for copy in made:
-        copy.wait_send()
-    for step in range(4):
+        value = mine_here[:, part * LANES : (part + 1) * LANES]
         for way in (0, 1):
-            for part in range(parts):
-                hop(way, step, part).wait_send()
+            value = value + z_in[3, way, part].astype(jnp.float32)
+        out_ref[:, lanes] = value.astype(out_ref.dtype)
+
+    drain((3,))
 
 
 def per_device(

time: 68.3 us -> 68.2 us (level)
  no operation moved by 1% of the time
where the time goes in v8:
time: 68.2 us; the launch traced here: 66.9 us
  Pallas kernels  63.9 us (94%)
  other arithmetic  1.69 us (2%)
  between operations  1.34 us (2%)
    pallas_call x1, Pallas kernels, per_device(): pl.pallas_call(kernel, out_shape=jax.ShapeDtypeStruct((rows, width), f32)...  63.9 us
    convert_element_type x1, other arithmetic, per_device(): return (residual.astype(f32) + gate_scale[None, :] * projected).astype(bf16)  1.69 us

profile of v8, /device:TPU:8, one launch (start us, length us, event | category | flops | bytes accessed | tf_op | source)
XLA Modules:
  0.0 66.9 jit_solution(7447516644300567153)
XLA Ops:
  1.3 0.0 copy-start
  1.3 0.0 copy-start.1
  1.3 63.9 %block.1 = f32[224,384]{1,0:T(8,128)} custom-call(bf16[224,384]{1,0:T(8,128)(2,1)} %q_hbm.1, bf16[224,384]{1,0:T(8,128)(2,1)} %k_hbm.1, bf16[224,384]{1,0:T(8,128)(2,1)} %v_hbm.1, bf16[1,1024,384]{2,1,0:T(8,128)(2,1)} %rk_hbm.1, bf16[1,1024,384]{2,1,0:T(8,128)(2,1)} %rv_hbm.1, s32[1,8]{1,0:T(1,128)} %lists.1, s32[1]{0:T(128)S(6)} %copy.12.counts, ...), custom_call_target="tpu_custom_call" | custom-call | tf_op jit(solution)/shard_map/block/pallas_call | solution.py:407
  65.2 0.0 copy-done
  65.2 0.0 copy-done.1
  65.2 1.7 %add_convert_fusion = bf16[224,384]{1,0:T(8,128)(2,1)} fusion(f32[224,384]{1,0:T(8,128)} %block.1, bf16[224,384]{1,0:T(8,128)(2,1)S(1)} %copy-done, f32[384]{0:T(512)S(1)} %copy-done.1), kind=kLoop, calls=%fused_computation | loop fusion | flops 344064 | bytes 689664 | tf_op jit(solution)/shard_map/convert_element_type | solution.py:443
Async XLA Ops:
  1.3 63.9 %copy-start = (bf16[224,384]{1,0:T(8,128)(2,1)S(1)}, bf16[224,384]{1,0:T(8,128)(2,1)}, u32[]{:S(2)}) copy-start(bf16[224,384]{1,0:T(8,128)(2,1)} %param.20) | copy-start | bytes 516100
  1.3 63.9 %copy-start.1 = (f32[384]{0:T(512)S(1)}, f32[384]{0:T(512)}, u32[]{:S(2)}) copy-start(f32[384]{0:T(512)} %param.21) | copy-start | bytes 4612
